TPU v7x, 512 devices: a whole 4x4x16 slice. The times are simulated.
512 devices in a mesh: freq: 16 (over y, x_lo, core), slab: 32 (over x_hi, z).
Axes of the slice: x: 4 (x_hi: 2, x_lo: 2; x = x_hi * 2 + x_lo), y: 4, z: 16, core: 2. Of those that a mesh axis runs over, the one named last changes fastest.
Arguments:
- forward_field: bfloat16 [16, 2, 12, 1310720], P('freq', None, None, 'slab'), may hold values from -6 to 6
- adjoint_field: bfloat16 [16, 2, 12, 1310720], P('freq', None, None, 'slab'), may hold values from -6 to 6
- mass_block: float32 [3, 4, 4], replicated, may hold values from -0.075 to 0.5
- cell_size: float32 [1310720], P('slab'), may hold values from 0.3 to 3
- freq_weight: float32 [64], replicated, may hold values from 0.05 to 0.2
- freq_ids: int32 [16], P('freq'), may hold values from 0 to 63, as said below
- receiver_cells: int32 [1024], replicated, may hold values from 0 to 1310719
- step_pairs: float32 [16, 3, 1310720], P(None, None, ('slab', 'freq'))
- grad_pairs: float32 [16, 3, 1310720], P(None, None, ('slab', 'freq')), as said below
Outputs:
- gradient: float32 [3, 1310720], P(None, ('slab', 'freq'))
- direction: float32 [3, 1310720], P(None, ('slab', 'freq'))
- predicted: float32 [16], replicated
Inputs may be any that keep to these rules, and one draw needn't show every extreme that they name: `freq_ids`: the slots hold distinct frequencies. `grad_pairs`: each gradient change has a positive inner product with its step.
All inputs are finite; a program needn't handle non-finite values.
Results may differ from a plain program's by a relative error of at most 0.0003.
Values sent between devices are 32-bit elements; how exact they have to be, the bound alone decides.
No kernel may reach another device: no remote copies, remote signals or barrier semaphores. Data moves between devices by JAX's collectives and lax.ppermute only.
A program may use at most 128 MiB of HBM per device.

v0:
```python
import jax
import jax.numpy as jnp
from jax import lax
from jax.sharding import PartitionSpec as P


def contract_slots(forward_field, adjoint_field, mass_block):
    slots = forward_field.shape[0]
    fwd = forward_field.astype(jnp.float32).reshape(slots, 2, 3, 4, -1)
    adj = adjoint_field.astype(jnp.float32).reshape(slots, 2, 3, 4, -1)
    coupled = jnp.einsum("kab,fpkbc->fpkac", mass_block, fwd, precision=lax.Precision.HIGHEST)
    return jnp.sum(adj[:, 0] * coupled[:, 0] - adj[:, 1] * coupled[:, 1], axis=2)


def solve_upper(upper, rhs):
    count = rhs.shape[0]
    places = jnp.arange(count, dtype=jnp.int32)
    result = jnp.zeros_like(rhs)
    for index in range(count - 1, -1, -1):
        value = (rhs[index] - jnp.sum(upper[index] * result)) / upper[index, index]
        result = jnp.where(places == index, value, result)
    return result


def solve_upper_transposed(upper, rhs):
    count = rhs.shape[0]
    places = jnp.arange(count, dtype=jnp.int32)
    result = jnp.zeros_like(rhs)
    for index in range(count):
        value = (rhs[index] - jnp.sum(upper[:, index] * result)) / upper[index, index]
        result = jnp.where(places == index, value, result)
    return result


def quasi_newton(gram, prod, precond, step_pairs, grad_pairs):
    count = step_pairs.shape[0]
    cross = gram[:count, count:]
    grad_gram = gram[count:, count:]
    upper = jnp.triu(cross)
    diagonal = jnp.diagonal(cross)
    gamma = cross[count - 1, count - 1] / grad_gram[count - 1, count - 1]
    first = solve_upper(upper, prod[:count])
    middle = (
        diagonal * first
        + gamma * jnp.dot(grad_gram, first, precision=lax.Precision.HIGHEST)
        - gamma * prod[count:]
    )
    second = solve_upper_transposed(upper, middle)
    along_steps = jnp.einsum("m,mkc->kc", second, step_pairs, precision=lax.Precision.HIGHEST)
    along_grads = jnp.einsum("m,mkc->kc", first, grad_pairs, precision=lax.Precision.HIGHEST)
    return -(gamma * precond + along_steps - gamma * along_grads)


def local(
    forward_field,
    adjoint_field,
    mass_block,
    cell_size,
    freq_weight,
    freq_ids,
    receiver_cells,
    step_pairs,
    grad_pairs,
):
    slots = forward_field.shape[0]
    cells = forward_field.shape[3]
    groups = lax.axis_size("freq")
    owned = cells // groups
    table = (
        freq_ids[:, None] == jnp.arange(freq_weight.shape[0], dtype=jnp.int32)[None, :]
    ).astype(jnp.float32)
    slot_weight = jnp.dot(table, freq_weight, precision=lax.Precision.HIGHEST)
    sens = (
        contract_slots(forward_field, adjoint_field, mass_block)
        * slot_weight[:, None, None]
        * cell_size[None, None, :]
    )
    gradient = lax.psum_scatter(jnp.sum(sens, axis=0), "freq", scatter_dimension=1, tiled=True)
    owner = lax.axis_index("slab") * groups + lax.axis_index("freq")
    offsets = receiver_cells - owner * owned
    hits = jnp.sum(
        offsets[:, None] == jnp.arange(owned, dtype=jnp.int32)[None, :], axis=0, dtype=jnp.int32
    )
    precond = gradient / (1.0 + 4.0 * hits.astype(jnp.float32))[None, :]
    count = step_pairs.shape[0]
    stacked = jnp.concatenate([step_pairs, grad_pairs], axis=0).reshape(2 * count, -1)
    gram_local = jnp.dot(stacked, stacked.T, precision=lax.Precision.HIGHEST)
    prod_local = jnp.dot(stacked, precond.reshape(-1), precision=lax.Precision.HIGHEST)
    gram = lax.psum(gram_local, ("freq", "slab"))
    prod = lax.psum(prod_local, ("freq", "slab"))
    direction = quasi_newton(gram, prod, precond, step_pairs, grad_pairs)
    slab_direction = lax.all_gather(direction, "freq", axis=1, tiled=True)
    own_terms = jnp.sum(sens * slab_direction[None], axis=(1, 2))
    partial_value = lax.dynamic_update_slice(
        jnp.zeros((slots * groups,), jnp.float32), own_terms, (lax.axis_index("freq") * slots,)
    )
    total_params = 3 * cells * lax.axis_size("slab")
    predicted = lax.psum(partial_value, ("freq", "slab")) / total_params
    return (gradient, direction, predicted)


def solution(mesh):
    in_specs = (
        P("freq", None, None, "slab"),
        P("freq", None, None, "slab"),
        P(),
        P("slab"),
        P(),
        P("freq"),
        P(),
        P(None, None, ("slab", "freq")),
        P(None, None, ("slab", "freq")),
    )
    out_specs = (P(None, ("slab", "freq")), P(None, ("slab", "freq")), P())
    return jax.shard_map(local, mesh=mesh, in_specs=in_specs, out_specs=out_specs, check_vma=False)
```

profile of v0, /device:TPU:1, one launch (start us, length us, event | category | flops | bytes accessed | tf_op | source)
XLA Modules:
  0.0 606.4 jit_solution(5428213809736995734)
XLA Ops:
  7.2 6.2 %fusion.55 = (f32[1,1,3,4,40960]{4,1,3,2,0:T(1,128)S(1)}, f32[1,1,3,4,40960]{4,1,3,2,0:T(1,128)S(1)}) fusion(bf16[1,2,3,4,40960]{4,1,3,2,0:T(2,128)(2,1)} %bitcast.197), kind=kLoop, calls=%fused_computation.156 | loop fusion | bytes 7864320 | tf_op jit(solution)/shard_map/slice | solution.py:12
  14.1 4.6 convolution_bitcast_fusion
  19.3 5.3 fusion.1
  25.5 10.0 %copy.28 = f32[3,40960]{0,1:T(8,128)} copy(f32[3,40960]{1,0:T(4,128)S(1)} %multiply_multiply_fusion) | data formatting | bytes 983040
  35.5 1.0 copy-done.4
  37.6 1.1 convert_reduce_fusion
  38.8 232.8 %reduce-scatter.4.cloned.1.call-done = f32[2560,3]{1,0:T(8,128)} async-done(((f32[40960,3]{1,0:T(8,128)}), f32[2560,3]{1,0:T(8,128)}) %reduce-scatter.4.cloned.1.call-update) | async-done | bytes 30736
  271.6 1.7 copy.29
  274.2 105.6 %all-reduce = (f32[32]{0:T(128)S(1)}, f32[32,32]{1,0:T(8,128)S(1)}) all-reduce(f32[32]{0:T(128)S(1)} %convolution_bitcast_fusion.3, f32[32,32]{1,0:T(8,128)S(1)} %convolution_bitcast_fusion.1), channel_id=1, replica_groups=mesh['freq'=16,'slab'=32] {'freq','slab'}, use_global_device_ids=true, to_apply=%region_4.0 | all-reduce | flops 1056 | bytes 8448 | tf_op jit(solution)/shard_map/psum | solution.py:90
  393.2 1.4 fusion.25
  396.5 1.4 fusion.27
  399.8 1.4 fusion.29
  403.1 1.4 fusion.31
  406.3 1.4 fusion.33
  409.6 1.4 fusion.35
  413.0 1.4 fusion.37
  416.2 1.3 fusion.39
  419.5 1.3 fusion.41
  422.7 1.3 fusion.43
  425.9 1.4 fusion.45
  429.2 1.4 fusion.47
  476.4 20.6 %all_gather.3 = f32[3,40960]{1,0:T(4,128)S(1)} all-gather(f32[3,2560]{1,0:T(4,128)S(1)} %fusion.7), channel_id=1, replica_groups=mesh['freq'=16,'slab'=32] {'freq'}, dimensions={1}, use_global_device_ids=true | all-gather | bytes 522240 | tf_op jit(solution)/shard_map/all_gather | solution.py:92
  497.0 1.6 multiply_reduce_fusion
  499.4 99.6 %psum.23 = f32[16]{0:T(128)S(1)} all-reduce(f32[16]{0:T(128)S(1)} %dynamic_update_slice.3), channel_id=1, replica_groups=mesh['freq'=16,'slab'=32] {'freq','slab'}, use_global_device_ids=true, to_apply=%region_38.39 | all-reduce | flops 16 | bytes 128 | tf_op jit(solution)/shard_map/psum | solution.py:98
  (65 shorter events, 22.4 us)
Async XLA Ops:
  7.2 6.9 %copy-start = (f32[3,4,4]{2,1,0:T(4,128)S(1)}, f32[3,4,4]{2,1,0:T(4,128)}, u32[]{:S(2)}) copy-start(f32[3,4,4]{2,1,0:T(4,128)} %param.11) | copy-start | bytes 580
  7.2 264.4 %reduce-scatter.4.cloned.1.call-start = ((), (), s32[]{:S(2)}) async-start(), calls=%async_computation.1 | async-start | bytes 22282240
  7.2 6.8 %copy-start.1 = (bf16[1,2,12,40960]{3,1,2,0:T(2,128)(2,1)S(1)}, bf16[1,2,12,40960]{3,1,2,0:T(2,128)(2,1)}, u32[]{:S(2)}) copy-start(bf16[1,2,12,40960]{3,1,2,0:T(2,128)(2,1)} %param.9) | copy-start | bytes 5898244
  14.1 4.6 copy-start.9
  19.3 5.3 copy-start.5
  35.5 1.0 copy-start.4
  35.5 1.2 copy-start.3
  36.5 1.1 copy-start.8
  273.3 223.7 %copy-start.6 = (f32[3,2560]{1,0:T(4,128)}, f32[3,2560]{1,0:T(4,128)S(1)}, u32[]{:S(2)}) copy-start(f32[3,2560]{1,0:T(4,128)S(1)} %copy.29) | copy-start | bytes 92164
  379.9 13.3 %copy-start.2 = (f32[16,16]{1,0:T(8,128)}, f32[16,16]{1,0:T(8,128)S(1)}, u32[]{:S(2)}) copy-start(f32[16,16]{1,0:T(8,128)S(1)} %get-tuple-element.52) | copy-start | bytes 3076
  476.4 123.1 %copy-start.7 = (f32[3,2560]{1,0:T(4,128)}, f32[3,2560]{1,0:T(4,128)S(1)}, u32[]{:S(2)}) copy-start(f32[3,2560]{1,0:T(4,128)S(1)} %fusion.7) | copy-start | bytes 92164
Sparse Core Ops, SparseCore 0:
  35.6 235.8 reduce-scatter.3
where the time goes:
time: 608 us; the launch traced here: 606 us
  waiting for transfers between devices  233 us (38%)
  blocking collectives  226 us (37%)
  between operations  77.7 us (13%)
  other arithmetic  39.5 us (6%)
  local copies, waits for them, and re-layouts  23.2 us (4%)
  matrix products  7.29 us (1%)
    unnamed x2, waiting for transfers between devices  233 us
    psum x1, blocking collectives, local(): prod = lax.psum(prod_local, ('freq', 'slab'))  106 us
    psum x1, blocking collectives, local(): predicted = lax.psum(partial_value, ('freq', 'slab')) / total_params  99.6 us
    all_gather x1, blocking collectives, local(): slab_direction = lax.all_gather(direction, 'freq', axis=1, tiled=True)  20.6 us
    reduce_sum x16, other arithmetic, solve_upper(): value = (rhs[index] - jnp.sum(upper[index] * result)) / upper[index, index]  18.9 us
    unnamed x23, local copies, waits for them, and re-layouts  12.9 us
  transfers between devices with their start and end apart: 1, of which 1 were waited for; matrix products, arithmetic and copies ran while one was open for 0% of the time, Pallas kernels for 0%

commit v1 on v0

v1 whole, which is shorter than its diff:
```python
import jax
import jax.numpy as jnp
from jax import lax
from jax.experimental import pallas as pl
from jax.experimental.pallas import tpu as pltpu
from jax.sharding import PartitionSpec as P

LANES = 128
PAIRS = 16
SLOTS = 16
EDGES = 12
GROUPS = 16
ROWS = 20
SLAB_ROWS = GROUPS * ROWS
PACK = 64
PER_STEP = 2
FREQ = ("y", "x_lo", "core")
PLANE = ("y", "x_lo", "core", "x_hi")
PARAMS_ALL = 3932160
HIGHEST = lax.Precision.HIGHEST


def sens_kernel(mass, weights, ids, fwd, adj, size, out, mixed):
    rows = PER_STEP * ROWS
    weight = weights[ids[0]]
    scale = size[...]
    for k in range(3):
        for first in range(0, 2 * rows, 16):
            span = slice(first, first + 16)
            e = [fwd[4 * k + b, span, :].astype(jnp.float32) for b in range(4)]
            total = None
            for a in range(4):
                coupled = mass[k * 16 + a * 4] * e[0]
                for b in range(1, 4):
                    coupled = coupled + mass[k * 16 + a * 4 + b] * e[b]
                term = adj[4 * k + a, span, :].astype(jnp.float32) * coupled
                total = term if total is None else total + term
            mixed[k, span, :] = total
        sens = mixed[k, pl.ds(0, rows, stride=2), :] - mixed[k, pl.ds(1, rows, stride=2), :]
        sens = (sens * weight) * scale
        for owner in range(PER_STEP):
            out[owner, k * ROWS : (k + 1) * ROWS, :] = sens[owner * ROWS : (owner + 1) * ROWS, :]


def sens_to_owners(fwd, adj, mass, size, weights, ids):
    smem = pl.BlockSpec(memory_space=pltpu.SMEM)
    rows = PER_STEP * ROWS
    field = pl.BlockSpec((EDGES, 2 * rows, LANES), lambda i: (0, i, 0))
    return pl.pallas_call(
        sens_kernel,
        grid=(GROUPS // PER_STEP,),
        out_shape=jax.ShapeDtypeStruct((GROUPS, PACK, LANES), jnp.float32),
        in_specs=[smem, smem, smem, field, field, pl.BlockSpec((rows, LANES), lambda i: (i, 0))],
        out_specs=pl.BlockSpec((PER_STEP, PACK, LANES), lambda i: (i, 0, 0)),
        scratch_shapes=[pltpu.VMEM((3, 2 * rows, LANES), jnp.float32)],
        compiler_params=pltpu.CompilerParams(vmem_limit_bytes=24 << 20),
        name="sens",
    )(mass, weights, ids, fwd, adj, size)


def products_kernel(cells, sens, steps, grads, gradient, precond, out):
    owner = lax.axis_index(("x_hi", "z")) * GROUPS + lax.axis_index(FREQ)
    offset = cells[...] - owner * (ROWS * LANES)
    inside = (offset >= 0) & (offset < ROWS * LANES)
    row = jnp.where(inside, offset >> 7, -1)
    lane = offset & (LANES - 1)
    row_hot, lane_hot = [], []
    for q in range(8):
        r = jnp.broadcast_to(row[q : q + 1, :], (24, LANES))
        c = jnp.broadcast_to(lane[q : q + 1, :], (LANES, LANES))
        row_hot.append((r == lax.broadcasted_iota(jnp.int32, r.shape, 0)).astype(jnp.float32))
        lane_hot.append((c == lax.broadcasted_iota(jnp.int32, c.shape, 0)).astype(jnp.float32))
    hits = lax.dot_general(
        jnp.concatenate(row_hot, axis=1).astype(jnp.bfloat16),
        jnp.concatenate(lane_hot, axis=1).astype(jnp.bfloat16),
        (((1,), (1,)), ((), ())),
        preferred_element_type=jnp.float32,
    )
    divisor = 1.0 + 4.0 * hits
    products = jnp.zeros((48, 40), jnp.float32)
    for k in range(3):
        slots, damped = [], []
        for r in range(ROWS):
            block = sens[pl.ds(k * ROWS + r, SLOTS, stride=PACK), :]
            span = slice(r * LANES, (r + 1) * LANES)
            total = jnp.sum(block, axis=0, keepdims=True)
            slots.append(block)
            damped.append(total / divisor[r : r + 1, :])
            gradient[k : k + 1, span] = total
            precond[k : k + 1, span] = damped[-1]
        pairs = jnp.concatenate([steps[k], grads[k]], axis=0)
        damped = jnp.broadcast_to(jnp.concatenate(damped, axis=1), (8, ROWS * LANES))
        products = products + lax.dot_general(
            jnp.concatenate([pairs, jnp.concatenate(slots, axis=1)], axis=0),
            jnp.concatenate([pairs, damped], axis=0),
            (((1,), (1,)), ((), ())),
            precision=HIGHEST,
            preferred_element_type=jnp.float32,
        )
    s, y, f = products[:16], products[16:32], products[32:]
    block = jnp.concatenate(
        [s[:, 16:32], y[:, 0:32], f[:, 0:32], s[:, 32:33], y[:, 32:33], f[:, 32:33], jnp.zeros((16, 45), jnp.float32)],
        axis=1,
    )
    for i in range(out.shape[0]):
        out[i] = block


def inner_products(cells, sens, steps, grads, copies):
    vmem = pl.BlockSpec(memory_space=pltpu.VMEM)
    own = jax.ShapeDtypeStruct((3, ROWS * LANES), jnp.float32)
    return pl.pallas_call(
        products_kernel,
        out_shape=(own, own, jax.ShapeDtypeStruct((copies, 16, LANES), jnp.float32)),
        in_specs=[vmem] * 4,
        out_specs=(vmem,) * 3,
        compiler_params=pltpu.CompilerParams(vmem_limit_bytes=24 << 20),
        name="products",
    )(cells, sens, steps, grads)


def resend_kernel(parts, out):
    total = jnp.sum(parts[...], axis=0)
    for i in range(out.shape[0]):
        out[i] = total


def resend(parts, copies):
    vmem = pl.BlockSpec(memory_space=pltpu.VMEM)
    return pl.pallas_call(
        resend_kernel,
        out_shape=jax.ShapeDtypeStruct((copies, 16, LANES), jnp.float32),
        in_specs=[vmem],
        out_specs=vmem,
        name="resend",
    )(parts)


def direction_kernel(parts, steps, grads, precond, direction, predicted):
    block = jnp.sum(parts[...], axis=0)
    row = lax.broadcasted_iota(jnp.int32, (16, LANES), 0)
    lane = lax.broadcasted_iota(jnp.int32, (16, LANES), 1)

    def column(i):
        return jnp.broadcast_to(block[:, i : i + 1], (16, LANES))

    def place(i, value, into):
        return jnp.where(row == i, jnp.broadcast_to(value, (16, LANES)), into)

    diagonal = jnp.sum(jnp.where(row == lane, block, 0.0), axis=1, keepdims=True)
    diagonal = jnp.broadcast_to(diagonal, (16, LANES))
    gamma = jnp.broadcast_to(diagonal[15:16, :] / column(47)[15:16, :], (16, LANES))
    rest = column(80)
    first = jnp.zeros((16, LANES), jnp.float32)
    along = jnp.zeros((16, LANES), jnp.float32)
    slots_first = jnp.zeros((16, LANES), jnp.float32)
    for m in range(15, -1, -1):
        value = rest[m : m + 1, :] / diagonal[m : m + 1, :]
        rest = rest - column(m) * value
        along = along + column(32 + m) * value
        slots_first = slots_first + column(64 + m) * value
        first = place(m, value, first)
    rest = diagonal * first + gamma * along - gamma * column(81)
    second = jnp.zeros((16, LANES), jnp.float32)
    slots_second = jnp.zeros((16, LANES), jnp.float32)
    for m in range(16):
        value = rest[m : m + 1, :] / diagonal[m : m + 1, :]
        rest = rest - column(16 + m) * value
        slots_second = slots_second + column(48 + m) * value
        second = place(m, value, second)
    change = -(gamma * column(82) + slots_second - gamma * slots_first) / PARAMS_ALL
    predicted[...] = jnp.sum(jnp.where(row == lane, change, 0.0), axis=0, keepdims=True)
    scaled = gamma * first
    for k in range(3):
        for r in range(ROWS):
            span = slice(r * LANES, (r + 1) * LANES)
            terms = second * steps[k, :, span] - scaled * grads[k, :, span]
            total = jnp.sum(terms, axis=0, keepdims=True)
            direction[k : k + 1, span] = -(gamma[0:1, :] * precond[k : k + 1, span] + total)


def directions(parts, steps, grads, precond):
    vmem = pl.BlockSpec(memory_space=pltpu.VMEM)
    return pl.pallas_call(
        direction_kernel,
        out_shape=(
            jax.ShapeDtypeStruct((3, ROWS * LANES), jnp.float32),
            jax.ShapeDtypeStruct((1, LANES), jnp.float32),
        ),
        in_specs=[vmem] * 4,
        out_specs=(vmem, vmem),
        name="direction",
    )(parts, steps, grads, precond)


def field_rows(field):
    split = field.reshape(2, EDGES, SLAB_ROWS, LANES)
    return split.transpose(1, 2, 0, 3).reshape(EDGES, 2 * SLAB_ROWS, LANES)


def local(
    forward_field,
    adjoint_field,
    mass_block,
    cell_size,
    freq_weight,
    freq_ids,
    receiver_cells,
    step_pairs,
    grad_pairs,
):
    steps = step_pairs.transpose(1, 0, 2)
    grads = grad_pairs.transpose(1, 0, 2)
    packed = sens_to_owners(
        field_rows(forward_field),
        field_rows(adjoint_field),
        mass_block.reshape(48),
        cell_size.reshape(SLAB_ROWS, LANES),
        freq_weight,
        freq_ids,
    )
    arrived = lax.all_to_all(packed, FREQ, 0, 0, tiled=True)
    gradient, precond, block = inner_products(
        receiver_cells.reshape(8, LANES),
        arrived.reshape(SLOTS * PACK, LANES),
        steps,
        grads,
        lax.axis_size(PLANE),
    )
    parts = lax.all_to_all(block, PLANE, 0, 0, tiled=True)
    parts = lax.all_to_all(resend(parts, lax.axis_size("z")), "z", 0, 0, tiled=True)
    direction, predicted = directions(parts, steps, grads, precond)
    return (gradient, direction, predicted[0, :SLOTS])


def solution(mesh):
    axes = ("y", "x_lo", "core", "x_hi", "z")
    parts = jax.sharding.Mesh(mesh.devices.reshape(4, 2, 2, 2, 16), axes)
    slab = ("x_hi", "z")
    owned = P(None, None, slab + FREQ)
    in_specs = (
        P(FREQ, None, None, slab),
        P(FREQ, None, None, slab),
        P(),
        P(slab),
        P(),
        P(FREQ),
        P(),
        owned,
        owned,
    )
    out_specs = (P(None, slab + FREQ), P(None, slab + FREQ), P())
    return jax.shard_map(local, mesh=parts, in_specs=in_specs, out_specs=out_specs, check_vma=False)
```

time: 608 us -> 76 us (0.12)
  the two profiles are of different devices: /device:TPU:1 before, /device:TPU:32 now
where the time goes in v1:
time: 76 us; the launch traced here: 75.6 us
  blocking collectives  58.8 us (77%)
  Pallas kernels  8.32 us (11%)
  local copies, waits for them, and re-layouts  7.14 us (9%)
  between operations  1.32 us (2%)
    all_to_all x1, blocking collectives, local(): lax.all_to_all(resend(parts, lax.axis_size('z')), 'z', 0, 0, tiled=True)  28.7 us
    all_to_all x1, blocking collectives, local(): arrived = lax.all_to_all(packed, FREQ, 0, 0, tiled=True)  16.2 us
    all_to_all x1, blocking collectives, local(): parts = lax.all_to_all(block, PLANE, 0, 0, tiled=True)  13.9 us
    unnamed x16, local copies, waits for them, and re-layouts  5.28 us
    pallas_call x1, Pallas kernels, sens_to_owners(): pl.pallas_call(sens_kernel, grid=(GROUPS // PER_STEP,), out_shape=jax.Sha...  2.54 us
    pallas_call x1, Pallas kernels, directions(): pl.pallas_call(direction_kernel, out_shape=(jax.ShapeDtypeStruct((3, ROWS...  2.31 us
    pallas_call x1, Pallas kernels, inner_products(): pl.pallas_call(products_kernel, out_shape=(own, own, jax.ShapeDtypeStruct...  1.84 us
    pallas_call x1, Pallas kernels, resend(): pl.pallas_call(resend_kernel, out_shape=jax.ShapeDtypeStruct((copies, 16,...  1.63 us

profile of v1, /device:TPU:32, one launch (start us, length us, event | category | flops | bytes accessed | tf_op | source)
XLA Modules:
  0.0 75.6 jit_solution(5098589619864282814)
XLA Ops:
  1.3 0.8 %reshape.31.mass = f32[48]{0:T(128)S(1)} reshape(f32[3,4,4]{2,1,0:T(4,128)} %param.11) | data formatting | bytes 384 | tf_op jit(solution)/shard_map/reshape | solution.py:217
  2.1 0.0 copy-start.2
  2.1 1.5 %copy-done.2 = bf16[1,2,12,40960]{3,1,2,0:T(2,128)(2,1)S(1)} copy-done((bf16[1,2,12,40960]{3,1,2,0:T(2,128)(2,1)S(1)}, bf16[1,2,12,40960]{3,1,2,0:T(2,128)(2,1)}, u32[]{:S(2)}) %copy-start.2) | copy-done | bytes 1966104
  3.6 0.0 copy-start.3
  3.6 1.5 %copy-done.3 = bf16[1,2,12,40960]{3,1,2,0:T(2,128)(2,1)S(1)} copy-done((bf16[1,2,12,40960]{3,1,2,0:T(2,128)(2,1)S(1)}, bf16[1,2,12,40960]{3,1,2,0:T(2,128)(2,1)}, u32[]{:S(2)}) %copy-start.3) | copy-done | bytes 1966104
  5.2 0.0 copy-start.4
  5.2 0.9 %copy-done.4 = f32[40960]{0:T(1024)S(1)} copy-done((f32[40960]{0:T(1024)S(1)}, f32[40960]{0:T(1024)}, u32[]{:S(2)}) %copy-start.4) | copy-done | bytes 163864
  6.1 0.0 copy-start.7
  6.1 0.7 copy-done.7
  6.7 0.0 copy-start
  6.7 0.0 copy-start.1
  6.7 2.5 %sens.1 = f32[16,64,128]{2,1,0:T(8,128)S(1)} custom-call(f32[48]{0:T(128)S(1)} %reshape.31.mass, f32[64]{0:T(128)S(1)} %copy-done.7, s32[1]{0:T(128)S(6)} %copy.14.ids, bf16[12,640,128]{2,1,0:T(8,128)(2,1)S(1)} %bitcast.22, bf16[12,640,128]{2,1,0:T(8,128)(2,1)S(1)} %bitcast.23, f32[320,128]{1,0:T(8,128)S(1)} %bitcast.24), custom_call_target="tpu_custom_call" | custom-call | tf_op jit(solution)/shard_map/sens/pallas_call | solution.py:49
  9.3 16.2 %all_to_all.15 = f32[16,64,128]{2,1,0:T(8,128)S(1)} all-to-all(f32[16,64,128]{2,1,0:T(8,128)S(1)} %sens.1), channel_id=1, replica_groups=mesh['y'=4,'x_lo'=2,'core'=2,'x_hi'=2,'z'=16] {'y','x_lo','core'}, dimensions={0} | all-to-all | bytes 1048576 | tf_op jit(solution)/shard_map/all_to_all | solution.py:222
  25.5 0.0 copy-done
  25.5 0.0 copy-done.1
  25.5 0.0 copy-done.6
  25.5 1.8 %products.1 = (f32[3,2560]{1,0:T(4,128)}, f32[3,2560]{1,0:T(4,128)S(1)}, f32[32,16,128]{2,1,0:T(8,128)S(1)}) custom-call(s32[8,128]{1,0:T(8,128)S(1)} %bitcast.25, f32[1024,128]{1,0:T(8,128)S(1)} %bitcast.17, f32[3,16,2560]{2,1,0:T(8,128)S(1)} %bitcast.19, f32[3,16,2560]{2,1,0:T(8,128)S(1)} %bitcast.21), custom_call_target="tpu_custom_call" | custom-call | tf_op jit(solution)/shard_map/products/pallas_call | solution.py:112
  27.3 0.0 copy-start.5
  27.3 0.6 copy-done.5
  27.9 13.9 %all_to_all.16.parts = f32[32,16,128]{2,1,0:T(8,128)} all-to-all(f32[32,16,128]{2,1,0:T(8,128)S(1)} %get-tuple-element.9), channel_id=1, replica_groups=mesh['y'=4,'x_lo'=2,'core'=2,'x_hi'=2,'z'=16] {'y','x_lo','core','x_hi'}, dimensions={0} | all-to-all | bytes 524288 | tf_op jit(solution)/shard_map/all_to_all | solution.py:230
  41.8 1.6 %resend.1 = f32[16,16,128]{2,1,0:T(8,128)} custom-call(f32[32,16,128]{2,1,0:T(8,128)} %all_to_all.16.parts), custom_call_target="tpu_custom_call" | custom-call | tf_op jit(solution)/shard_map/resend/pallas_call | solution.py:130
  43.5 28.7 %all_to_all.17.parts = f32[16,16,128]{2,1,0:T(8,128)} all-to-all(f32[16,16,128]{2,1,0:T(8,128)} %resend.1), channel_id=1, replica_groups=mesh['y'=4,'x_lo'=2,'core'=2,'x_hi'=2,'z'=16] {'z'}, dimensions={0} | all-to-all | bytes 262144 | tf_op jit(solution)/shard_map/all_to_all | solution.py:231
  72.2 2.3 %direction.1 = (f32[3,2560]{1,0:T(4,128)}, f32[1,128]{1,0:T(1,128)}) custom-call(f32[16,16,128]{2,1,0:T(8,128)} %all_to_all.17.parts, f32[3,16,2560]{2,1,0:T(8,128)} %bitcast.18, f32[3,16,2560]{2,1,0:T(8,128)} %bitcast.20, f32[3,2560]{1,0:T(4,128)} %copy-done.5), custom_call_target="tpu_custom_call" | custom-call | tf_op jit(solution)/shard_map/direction/pallas_call | solution.py:184
  74.5 1.1 %slice_bitcast_fusion = f32[16]{0:T(128)} fusion(f32[1,128]{1,0:T(1,128)} %get-tuple-element.12), kind=kLoop, calls=%fused_computation | loop fusion | bytes 128 | tf_op jit(solution)/shard_map/squeeze | solution.py:233
  (1 shorter events, 0.0 us)
Async XLA Ops:
  2.1 1.6 %copy-start.2 = (bf16[1,2,12,40960]{3,1,2,0:T(2,128)(2,1)S(1)}, bf16[1,2,12,40960]{3,1,2,0:T(2,128)(2,1)}, u32[]{:S(2)}) copy-start(bf16[1,2,12,40960]{3,1,2,0:T(2,128)(2,1)} %param.9) | copy-start | bytes 5898244
  3.6 1.5 %copy-start.3 = (bf16[1,2,12,40960]{3,1,2,0:T(2,128)(2,1)S(1)}, bf16[1,2,12,40960]{3,1,2,0:T(2,128)(2,1)}, u32[]{:S(2)}) copy-start(bf16[1,2,12,40960]{3,1,2,0:T(2,128)(2,1)} %param.10) | copy-start | bytes 5898244
  5.2 0.9 %copy-start.4 = (f32[40960]{0:T(1024)S(1)}, f32[40960]{0:T(1024)}, u32[]{:S(2)}) copy-start(f32[40960]{0:T(1024)} %param.12) | copy-start | bytes 491524
  6.1 0.7 copy-start.7
  6.7 18.7 %copy-start = (f32[16,3,2560]{2,0,1:T(8,128)S(1)}, f32[16,3,2560]{2,0,1:T(8,128)}, u32[]{:S(2)}) copy-start(f32[16,3,2560]{2,0,1:T(8,128)} %param.16) | copy-start | bytes 1474564
  6.7 18.7 %copy-start.1 = (f32[16,3,2560]{2,0,1:T(8,128)S(1)}, f32[16,3,2560]{2,0,1:T(8,128)}, u32[]{:S(2)}) copy-start(f32[16,3,2560]{2,0,1:T(8,128)} %param.17) | copy-start | bytes 1474564
  6.7 18.7 %copy-start.6 = (s32[1024]{0:T(1024)S(1)}, s32[1024]{0:T(1024)}, u32[]{:S(2)}) copy-start(s32[1024]{0:T(1024)} %param.15) | copy-start | bytes 12292
  27.3 0.6 copy-start.5

commit v2 on v1

v2 whole, which is shorter than its diff:
```python
import jax
import jax.numpy as jnp
from jax import lax
from jax.experimental import pallas as pl
from jax.experimental.pallas import tpu as pltpu
from jax.sharding import PartitionSpec as P

LANES = 128
PAIRS = 16
SLOTS = 16
EDGES = 12
GROUPS = 16
ROWS = 20
SLAB_ROWS = GROUPS * ROWS
PACK = 64
PER_STEP = 4
FREQ = ("y", "x_lo", "core")
PLANE = ("y", "x_lo", "core", "x_hi")
PARAMS_ALL = 3932160
HIGHEST = lax.Precision.HIGHEST


def sens_kernel(
    ids,
    mass_in,
    weights_in,
    fwd,
    adj,
    size,
    out,
    mass,
    weights,
    e_buf,
    l_buf,
    scale_buf,
    mixed,
    e_sem,
    l_sem,
    small_sem,
):
    rows = PER_STEP * ROWS
    steps = GROUPS // PER_STEP
    small = [
        pltpu.make_async_copy(mass_in, mass, small_sem.at[0]),
        pltpu.make_async_copy(weights_in, weights, small_sem.at[1]),
        pltpu.make_async_copy(size, scale_buf, small_sem.at[2]),
    ]

    def copies(i):
        span = pl.ds(pl.multiple_of(i * 2 * rows, 2 * rows), 2 * rows)
        return (
            pltpu.make_async_copy(fwd.at[:, span, :], e_buf.at[:, span, :], e_sem.at[i]),
            pltpu.make_async_copy(adj.at[:, span, :], l_buf.at[:, span, :], l_sem.at[i]),
        )

    for copy in small:
        copy.start()
    for i in range(steps):
        for copy in copies(i):
            copy.start()
    for copy in small:
        copy.wait()
    weight = weights[ids[0]]

    @pl.loop(0, steps)
    def _(i):
        for copy in copies(i):
            copy.wait()
        scale = scale_buf[pl.ds(pl.multiple_of(i * rows, 8), rows), :]
        for k in range(3):
            for first in range(0, 2 * rows, 16):
                span = pl.ds(pl.multiple_of(i * 2 * rows + first, 16), 16)
                e = [e_buf[4 * k + b, span, :].astype(jnp.float32) for b in range(4)]
                total = None
                for a in range(4):
                    coupled = mass[k, a, 0] * e[0]
                    for b in range(1, 4):
                        coupled = coupled + mass[k, a, b] * e[b]
                    term = l_buf[4 * k + a, span, :].astype(jnp.float32) * coupled
                    total = term if total is None else total + term
                mixed[k, first : first + 16, :] = total
            sens = mixed[k, pl.ds(0, rows, stride=2), :] - mixed[k, pl.ds(1, rows, stride=2), :]
            sens = (sens * weight) * scale
            for owner in range(PER_STEP):
                out[i * PER_STEP + owner, k * ROWS : (k + 1) * ROWS, :] = sens[owner * ROWS : (owner + 1) * ROWS, :]


def sens_to_owners(fwd, adj, mass, size, weights, ids):
    smem = pl.BlockSpec(memory_space=pltpu.SMEM)
    hbm = pl.BlockSpec(memory_space=pltpu.HBM)
    rows = PER_STEP * ROWS
    steps = GROUPS // PER_STEP
    return pl.pallas_call(
        sens_kernel,
        out_shape=jax.ShapeDtypeStruct((GROUPS, PACK, LANES), jnp.float32),
        in_specs=[smem, hbm, hbm, hbm, hbm, hbm],
        out_specs=pl.BlockSpec(memory_space=pltpu.VMEM),
        scratch_shapes=[
            pltpu.SMEM(mass.shape, mass.dtype),
            pltpu.SMEM(weights.shape, weights.dtype),
            pltpu.VMEM(fwd.shape, fwd.dtype),
            pltpu.VMEM(adj.shape, adj.dtype),
            pltpu.VMEM(size.shape, size.dtype),
            pltpu.VMEM((3, 2 * rows, LANES), jnp.float32),
            pltpu.SemaphoreType.DMA((steps,)),
            pltpu.SemaphoreType.DMA((steps,)),
            pltpu.SemaphoreType.DMA((3,)),
        ],
        compiler_params=pltpu.CompilerParams(vmem_limit_bytes=12 << 20),
        name="sens",
    )(ids, *[pltpu.with_memory_space_constraint(each, pltpu.HBM) for each in (mass, weights, fwd, adj, size)])


def products_kernel(cells, sens, steps, grads, gradient_out, precond, out, gradient, gradient_sem):
    owner = lax.axis_index(("x_hi", "z")) * GROUPS + lax.axis_index(FREQ)
    offset = cells[...] - owner * (ROWS * LANES)
    inside = (offset >= 0) & (offset < ROWS * LANES)
    row = jnp.where(inside, offset >> 7, -1)
    lane = offset & (LANES - 1)
    row_hot, lane_hot = [], []
    for q in range(8):
        r = jnp.broadcast_to(row[q : q + 1, :], (24, LANES))
        c = jnp.broadcast_to(lane[q : q + 1, :], (LANES, LANES))
        row_hot.append((r == lax.broadcasted_iota(jnp.int32, r.shape, 0)).astype(jnp.float32))
        lane_hot.append((c == lax.broadcasted_iota(jnp.int32, c.shape, 0)).astype(jnp.float32))
    hits = lax.dot_general(
        jnp.concatenate(row_hot, axis=1).astype(jnp.bfloat16),
        jnp.concatenate(lane_hot, axis=1).astype(jnp.bfloat16),
        (((1,), (1,)), ((), ())),
        preferred_element_type=jnp.float32,
    )
    divisor = 1.0 + 4.0 * hits
    products = jnp.zeros((48, 40), jnp.float32)
    gradient_copy = pltpu.make_async_copy(gradient, gradient_out, gradient_sem)
    for k in range(3):
        slots, damped = [], []
        for r in range(ROWS):
            block = sens[pl.ds(k * ROWS + r, SLOTS, stride=PACK), :]
            span = slice(r * LANES, (r + 1) * LANES)
            total = jnp.sum(block, axis=0, keepdims=True)
            slots.append(block)
            damped.append(total / divisor[r : r + 1, :])
            gradient[k : k + 1, span] = total
            precond[k : k + 1, span] = damped[-1]
        if k == 2:
            gradient_copy.start()
        pairs = jnp.concatenate([steps[k], grads[k]], axis=0)
        damped = jnp.broadcast_to(jnp.concatenate(damped, axis=1), (8, ROWS * LANES))
        products = products + lax.dot_general(
            jnp.concatenate([pairs, jnp.concatenate(slots, axis=1)], axis=0),
            jnp.concatenate([pairs, damped], axis=0),
            (((1,), (1,)), ((), ())),
            precision=HIGHEST,
            preferred_element_type=jnp.float32,
        )
    s, y, f = products[:16], products[16:32], products[32:]
    row = lax.broadcasted_iota(jnp.int32, (16, 16), 0)
    lane = lax.broadcasted_iota(jnp.int32, (16, 16), 1)
    grad_gram = y[:, 16:32]
    block = jnp.concatenate(
        [
            jnp.where(row <= lane, s[:, 16:32], grad_gram),
            jnp.sum(jnp.where(row == lane, grad_gram, 0.0), axis=1, keepdims=True),
            f[:, 0:32],
            s[:, 32:33],
            y[:, 32:33],
            f[:, 32:33],
            jnp.zeros((16, 12), jnp.float32),
        ],
        axis=1,
    )
    block = jnp.concatenate([block[:8], block[8:]], axis=1)
    for i in range(out.shape[0]):
        out[i] = block
    gradient_copy.wait()


def inner_products(cells, sens, steps, grads, copies):
    vmem = pl.BlockSpec(memory_space=pltpu.VMEM)
    own = jax.ShapeDtypeStruct((3, ROWS * LANES), jnp.float32)
    return pl.pallas_call(
        products_kernel,
        out_shape=(own, own, jax.ShapeDtypeStruct((copies, 8, LANES), jnp.float32)),
        in_specs=[vmem] * 4,
        out_specs=(pl.BlockSpec(memory_space=pltpu.HBM), vmem, vmem),
        scratch_shapes=[pltpu.VMEM(own.shape, own.dtype), pltpu.SemaphoreType.DMA(())],
        compiler_params=pltpu.CompilerParams(vmem_limit_bytes=12 << 20),
        name="products",
    )(cells, sens, steps, grads)


def resend_kernel(parts, out):
    total = jnp.sum(parts[...], axis=0)
    for i in range(out.shape[0]):
        out[i] = total


def resend(parts, copies):
    vmem = pl.BlockSpec(memory_space=pltpu.VMEM)
    return pl.pallas_call(
        resend_kernel,
        out_shape=jax.ShapeDtypeStruct((copies, 8, LANES), jnp.float32),
        in_specs=[vmem],
        out_specs=vmem,
        compiler_params=pltpu.CompilerParams(vmem_limit_bytes=4 << 20),
        name="resend",
    )(parts)


def direction_kernel(parts, steps, grads, precond, direction, predicted):
    halves = jnp.sum(parts[...], axis=0)
    block = jnp.concatenate([halves[:, :64], halves[:, 64:]], axis=0)
    turned = jnp.concatenate([block, jnp.zeros((16, 64), jnp.float32)], axis=1)
    turned = jnp.concatenate([turned, jnp.zeros((LANES - 16, LANES), jnp.float32)], axis=0).T[:16]
    row = lax.broadcasted_iota(jnp.int32, (16, LANES), 0)
    lane = lax.broadcasted_iota(jnp.int32, (16, LANES), 1)

    def column(i, of=block):
        return jnp.broadcast_to(of[:, i : i + 1], (16, LANES))

    def place(i, value, into):
        return jnp.where(row == i, jnp.broadcast_to(value, (16, LANES)), into)

    diagonal = jnp.where(row[:, :64] == lane[:, :64], block, 0.0)
    diagonal = jnp.broadcast_to(jnp.sum(diagonal, axis=1, keepdims=True), (16, LANES))
    grad_diagonal = column(16)
    gamma = jnp.broadcast_to(diagonal[15:16, :] / grad_diagonal[15:16, :], (16, LANES))
    rest = column(49)
    first = jnp.zeros((16, LANES), jnp.float32)
    along = jnp.zeros((16, LANES), jnp.float32)
    slots_first = jnp.zeros((16, LANES), jnp.float32)
    for m in range(15, -1, -1):
        value = rest[m : m + 1, :] / diagonal[m : m + 1, :]
        upper = column(m)
        rest = rest - upper * value
        grad_column = jnp.where(row > m, upper, jnp.where(row < m, column(m, turned), grad_diagonal))
        along = along + grad_column * value
        slots_first = slots_first + column(33 + m) * value
        first = place(m, value, first)
    rest = diagonal * first + gamma * along - gamma * column(50)
    second = jnp.zeros((16, LANES), jnp.float32)
    slots_second = jnp.zeros((16, LANES), jnp.float32)
    for m in range(16):
        value = rest[m : m + 1, :] / diagonal[m : m + 1, :]
        rest = rest - column(m, turned) * value
        slots_second = slots_second + column(17 + m) * value
        second = place(m, value, second)
    change = -(gamma * column(51) + slots_second - gamma * slots_first) / PARAMS_ALL
    predicted[...] = jnp.sum(jnp.where(row == lane, change, 0.0), axis=0)[:SLOTS]
    scaled = gamma * first
    for k in range(3):
        for r in range(ROWS):
            span = slice(r * LANES, (r + 1) * LANES)
            terms = second * steps[k, :, span] - scaled * grads[k, :, span]
            total = jnp.sum(terms, axis=0, keepdims=True)
            direction[k : k + 1, span] = -(gamma[0:1, :] * precond[k : k + 1, span] + total)


def directions(parts, steps, grads, precond):
    vmem = pl.BlockSpec(memory_space=pltpu.VMEM)
    return pl.pallas_call(
        direction_kernel,
        out_shape=(
            jax.ShapeDtypeStruct((3, ROWS * LANES), jnp.float32),
            jax.ShapeDtypeStruct((SLOTS,), jnp.float32),
        ),
        in_specs=[vmem] * 4,
        out_specs=(vmem, vmem),
        compiler_params=pltpu.CompilerParams(vmem_limit_bytes=8 << 20),
        name="direction",
    )(parts, steps, grads, precond)


def field_rows(field):
    split = field.reshape(2, EDGES, SLAB_ROWS, LANES)
    return split.transpose(1, 2, 0, 3).reshape(EDGES, 2 * SLAB_ROWS, LANES)


def local(
    forward_field,
    adjoint_field,
    mass_block,
    cell_size,
    freq_weight,
    freq_ids,
    receiver_cells,
    step_pairs,
    grad_pairs,
):
    steps = step_pairs.transpose(1, 0, 2)
    grads = grad_pairs.transpose(1, 0, 2)
    packed = sens_to_owners(
        field_rows(forward_field),
        field_rows(adjoint_field),
        mass_block,
        cell_size.reshape(SLAB_ROWS, LANES),
        freq_weight,
        freq_ids,
    )
    arrived = lax.all_to_all(packed, FREQ, 0, 0, tiled=True)
    gradient, precond, block = inner_products(
        receiver_cells.reshape(8, LANES),
        arrived.reshape(SLOTS * PACK, LANES),
        steps,
        grads,
        lax.axis_size(PLANE),
    )
    parts = lax.all_to_all(block, PLANE, 0, 0, tiled=True)
    parts = lax.all_to_all(resend(parts, lax.axis_size("z")), "z", 0, 0, tiled=True)
    direction, predicted = directions(parts, steps, grads, precond)
    return (gradient, direction, predicted)


def solution(mesh):
    axes = ("y", "x_lo", "core", "x_hi", "z")
    parts = jax.sharding.Mesh(mesh.devices.reshape(4, 2, 2, 2, 16), axes)
    slab = ("x_hi", "z")
    owned = P(None, None, slab + FREQ)
    in_specs = (
        P(FREQ, None, None, slab),
        P(FREQ, None, None, slab),
        P(),
        P(slab),
        P(),
        P(FREQ),
        P(),
        owned,
        owned,
    )
    out_specs = (P(None, slab + FREQ), P(None, slab + FREQ), P())
    return jax.shard_map(local, mesh=parts, in_specs=in_specs, out_specs=out_specs, check_vma=False)
```

time: 76 us -> 63.9 us (0.84)
  the two profiles are of different devices: /device:TPU:32 before, /device:TPU:1 now
where the time goes in v2:
time: 63.9 us; the launch traced here: 63.7 us
  blocking collectives  55.7 us (87%)
  Pallas kernels  6.68 us (10%)
  between operations  1.32 us (2%)
    all_to_all x1, blocking collectives, local(): lax.all_to_all(resend(parts, lax.axis_size('z')), 'z', 0, 0, tiled=True)  25.1 us
    all_to_all x1, blocking collectives, local(): arrived = lax.all_to_all(packed, FREQ, 0, 0, tiled=True)  19.2 us
    all_to_all x1, blocking collectives, local(): parts = lax.all_to_all(block, PLANE, 0, 0, tiled=True)  11.4 us
    pallas_call x1, Pallas kernels, sens_to_owners(): pl.pallas_call(sens_kernel, out_shape=jax.ShapeDtypeStruct((GROUPS, PACK,...  3.52 us
    pallas_call x1, Pallas kernels, inner_products(): pl.pallas_call(products_kernel, out_shape=(own, own, jax.ShapeDtypeStruct...  1.98 us

profile of v2, /device:TPU:1, one launch (start us, length us, event | category | flops | bytes accessed | tf_op | source)
XLA Modules:
  0.0 63.7 jit_solution(9766064577377131654)
XLA Ops:
  1.3 0.0 copy-start
  1.3 0.0 copy-start.1
  1.3 0.0 copy-start.2
  1.3 3.5 %sens.1 = f32[16,64,128]{2,1,0:T(8,128)S(1)} custom-call(s32[1]{0:T(128)S(6)} %copy.14.ids, f32[3,4,4]{2,1,0:T(4,128)} %mass_in.1, f32[64]{0:T(128)} %weights_in.1, bf16[12,640,128]{2,1,0:T(8,128)(2,1)} %bitcast.21, bf16[12,640,128]{2,1,0:T(8,128)(2,1)} %bitcast.22, f32[320,128]{1,0:T(8,128)} %bitcast.23), custom_call_target="tpu_custom_call" | custom-call | tf_op jit(solution)/shard_map/sens/pallas_call | solution.py:93
  4.8 19.2 %all_to_all.15 = f32[16,64,128]{2,1,0:T(8,128)S(1)} all-to-all(f32[16,64,128]{2,1,0:T(8,128)S(1)} %sens.1), channel_id=1, replica_groups=mesh['y'=4,'x_lo'=2,'core'=2,'x_hi'=2,'z'=16] {'y','x_lo','core'}, dimensions={0} | all-to-all | bytes 1048576 | tf_op jit(solution)/shard_map/all_to_all | solution.py:300
  24.0 0.0 copy-done
  24.0 0.0 copy-done.1
  24.0 0.0 copy-done.2
  24.0 2.0 %products.1 = (f32[3,2560]{1,0:T(4,128)}, f32[3,2560]{1,0:T(4,128)S(1)}, f32[32,8,128]{2,1,0:T(8,128)S(1)}) custom-call(s32[8,128]{1,0:T(8,128)S(1)} %bitcast.20, f32[1024,128]{1,0:T(8,128)S(1)} %bitcast.15, f32[3,16,2560]{2,1,0:T(8,128)S(1)} %bitcast.16, f32[3,16,2560]{2,1,0:T(8,128)S(1)} %bitcast.18), custom_call_target="tpu_custom_call" | custom-call | tf_op jit(solution)/shard_map/products/pallas_call | solution.py:181
  26.0 11.4 %all_to_all.16.parts = f32[32,8,128]{2,1,0:T(8,128)S(1)} all-to-all(f32[32,8,128]{2,1,0:T(8,128)S(1)} %get-tuple-element.9), channel_id=1, replica_groups=mesh['y'=4,'x_lo'=2,'core'=2,'x_hi'=2,'z'=16] {'y','x_lo','core','x_hi'}, dimensions={0} | all-to-all | bytes 262144 | tf_op jit(solution)/shard_map/all_to_all | solution.py:308
  37.5 25.1 %all_to_all.17.parts = f32[16,8,128]{2,1,0:T(8,128)S(1)} all-to-all(f32[16,8,128]{2,1,0:T(8,128)S(1)} %resend.1), channel_id=1, replica_groups=mesh['y'=4,'x_lo'=2,'core'=2,'x_hi'=2,'z'=16] {'z'}, dimensions={0} | all-to-all | bytes 131072 | tf_op jit(solution)/shard_map/all_to_all | solution.py:309
  62.6 1.1 %direction.1 = (f32[3,2560]{1,0:T(4,128)}, f32[16]{0:T(128)}) custom-call(f32[16,8,128]{2,1,0:T(8,128)S(1)} %all_to_all.17.parts, f32[3,16,2560]{2,1,0:T(8,128)S(1)} %bitcast.17, f32[3,16,2560]{2,1,0:T(8,128)S(1)} %bitcast.19, f32[3,2560]{1,0:T(4,128)S(1)} %get-tuple-element.10.precond), custom_call_target="tpu_custom_call" | custom-call | tf_op jit(solution)/shard_map/direction/pallas_call | solution.py:261
  (1 shorter events, 0.0 us)
Async XLA Ops:
  1.3 22.8 %copy-start = (f32[16,3,2560]{2,0,1:T(8,128)S(1)}, f32[16,3,2560]{2,0,1:T(8,128)}, u32[]{:S(2)}) copy-start(f32[16,3,2560]{2,0,1:T(8,128)} %param.16) | copy-start | bytes 1474564
  1.3 22.8 %copy-start.1 = (f32[16,3,2560]{2,0,1:T(8,128)S(1)}, f32[16,3,2560]{2,0,1:T(8,128)}, u32[]{:S(2)}) copy-start(f32[16,3,2560]{2,0,1:T(8,128)} %param.17) | copy-start | bytes 1474564
  1.3 22.7 %copy-start.2 = (s32[1024]{0:T(1024)S(1)}, s32[1024]{0:T(1024)}, u32[]{:S(2)}) copy-start(s32[1024]{0:T(1024)} %param.15) | copy-start | bytes 12292

commit v3 on v2

--- a/solution.py
+++ b/solution.py
@@ -306,7 +306,7 @@
         lax.axis_size(PLANE),
     )
     parts = lax.all_to_all(block, PLANE, 0, 0, tiled=True)
-    parts = lax.all_to_all(resend(parts, lax.axis_size("z")), "z", 0, 0, tiled=True)
+    parts = lax.all_to_all(resend(parts, lax.axis_size("z")), "z", 0, 0, tiled=True, axis_index_groups=[[(i+8)%16 for i in range(16)]])
     direction, predicted = directions(parts, steps, grads, precond)
     return (gradient, direction, predicted)
 

time: 63.9 us -> 58.9 us (0.922)
  blocking collectives: 55.7 us -> 50.6 us
    all_to_all x1, blocking collectives: 25.1 us -> 20.1 us  [local(): lax.all_to_all(resend(parts, lax.axis_size('z')), 'z', 0, 0, tiled=True,...]
where the time goes in v3:
time: 58.9 us; the launch traced here: 58.7 us
  blocking collectives  50.6 us (86%)
  Pallas kernels  6.68 us (11%)
  between operations  1.32 us (2%)
    all_to_all x1, blocking collectives, local(): lax.all_to_all(resend(parts, lax.axis_size('z')), 'z', 0, 0, tiled=True,...  20.1 us
    all_to_all x1, blocking collectives, local(): arrived = lax.all_to_all(packed, FREQ, 0, 0, tiled=True)  19.2 us
    all_to_all x1, blocking collectives, local(): parts = lax.all_to_all(block, PLANE, 0, 0, tiled=True)  11.4 us
    pallas_call x1, Pallas kernels, sens_to_owners(): pl.pallas_call(sens_kernel, out_shape=jax.ShapeDtypeStruct((GROUPS, PACK,...  3.52 us
    pallas_call x1, Pallas kernels, inner_products(): pl.pallas_call(products_kernel, out_shape=(own, own, jax.ShapeDtypeStruct...  1.98 us

profile of v3, /device:TPU:1, one launch (start us, length us, event | category | flops | bytes accessed | tf_op | source)
XLA Modules:
  0.0 58.7 jit_solution(1689364635391628833)
XLA Ops:
  1.3 0.0 copy-start
  1.3 0.0 copy-start.1
  1.3 0.0 copy-start.2
  1.3 3.5 %sens.1 = f32[16,64,128]{2,1,0:T(8,128)S(1)} custom-call(s32[1]{0:T(128)S(6)} %copy.14.ids, f32[3,4,4]{2,1,0:T(4,128)} %mass_in.1, f32[64]{0:T(128)} %weights_in.1, bf16[12,640,128]{2,1,0:T(8,128)(2,1)} %bitcast.21, bf16[12,640,128]{2,1,0:T(8,128)(2,1)} %bitcast.22, f32[320,128]{1,0:T(8,128)} %bitcast.23), custom_call_target="tpu_custom_call" | custom-call | tf_op jit(solution)/shard_map/sens/pallas_call | solution.py:93
  4.8 19.2 %all_to_all.15 = f32[16,64,128]{2,1,0:T(8,128)S(1)} all-to-all(f32[16,64,128]{2,1,0:T(8,128)S(1)} %sens.1), channel_id=1, replica_groups=mesh['y'=4,'x_lo'=2,'core'=2,'x_hi'=2,'z'=16] {'y','x_lo','core'}, dimensions={0} | all-to-all | bytes 1048576 | tf_op jit(solution)/shard_map/all_to_all | solution.py:300
  24.0 0.0 copy-done
  24.0 0.0 copy-done.1
  24.0 0.0 copy-done.2
  24.0 2.0 %products.1 = (f32[3,2560]{1,0:T(4,128)}, f32[3,2560]{1,0:T(4,128)S(1)}, f32[32,8,128]{2,1,0:T(8,128)S(1)}) custom-call(s32[8,128]{1,0:T(8,128)S(1)} %bitcast.20, f32[1024,128]{1,0:T(8,128)S(1)} %bitcast.15, f32[3,16,2560]{2,1,0:T(8,128)S(1)} %bitcast.16, f32[3,16,2560]{2,1,0:T(8,128)S(1)} %bitcast.18), custom_call_target="tpu_custom_call" | custom-call | tf_op jit(solution)/shard_map/products/pallas_call | solution.py:181
  26.0 11.4 %all_to_all.16.parts = f32[32,8,128]{2,1,0:T(8,128)S(1)} all-to-all(f32[32,8,128]{2,1,0:T(8,128)S(1)} %get-tuple-element.9), channel_id=1, replica_groups=mesh['y'=4,'x_lo'=2,'core'=2,'x_hi'=2,'z'=16] {'y','x_lo','core','x_hi'}, dimensions={0} | all-to-all | bytes 262144 | tf_op jit(solution)/shard_map/all_to_all | solution.py:308
  37.5 20.1 %all_to_all.17.parts = f32[16,8,128]{2,1,0:T(8,128)S(1)} all-to-all(f32[16,8,128]{2,1,0:T(8,128)S(1)} %resend.1), channel_id=1, replica_groups={{8,9,10,11,12,13,14,15,0,1,2,3,4,5,6,7},{24,25,26,27,28,29,30,31,16,17,..., dimensions={0} | all-to-all | bytes 131072 | tf_op jit(solution)/shard_map/all_to_all | solution.py:309
  57.5 1.1 %direction.1 = (f32[3,2560]{1,0:T(4,128)}, f32[16]{0:T(128)}) custom-call(f32[16,8,128]{2,1,0:T(8,128)S(1)} %all_to_all.17.parts, f32[3,16,2560]{2,1,0:T(8,128)S(1)} %bitcast.17, f32[3,16,2560]{2,1,0:T(8,128)S(1)} %bitcast.19, f32[3,2560]{1,0:T(4,128)S(1)} %get-tuple-element.10.precond), custom_call_target="tpu_custom_call" | custom-call | tf_op jit(solution)/shard_map/direction/pallas_call | solution.py:261
  (1 shorter events, 0.0 us)
Async XLA Ops:
  1.3 22.8 %copy-start = (f32[16,3,2560]{2,0,1:T(8,128)S(1)}, f32[16,3,2560]{2,0,1:T(8,128)}, u32[]{:S(2)}) copy-start(f32[16,3,2560]{2,0,1:T(8,128)} %param.16) | copy-start | bytes 1474564
  1.3 22.8 %copy-start.1 = (f32[16,3,2560]{2,0,1:T(8,128)S(1)}, f32[16,3,2560]{2,0,1:T(8,128)}, u32[]{:S(2)}) copy-start(f32[16,3,2560]{2,0,1:T(8,128)} %param.17) | copy-start | bytes 1474564
  1.3 22.7 %copy-start.2 = (s32[1024]{0:T(1024)S(1)}, s32[1024]{0:T(1024)}, u32[]{:S(2)}) copy-start(s32[1024]{0:T(1024)} %param.15) | copy-start | bytes 12292

commit v4 on v3

--- a/solution.py
+++ b/solution.py
@@ -17,7 +17,7 @@
 FREQ = ("y", "x_lo", "core")
 PLANE = ("y", "x_lo", "core", "x_hi")
 PARAMS_ALL = 3932160
-HIGHEST = lax.Precision.HIGHEST
+SPLITS = 3
 
 
 def sens_kernel(
@@ -66,7 +66,7 @@
     def _(i):
         for copy in copies(i):
             copy.wait()
-        scale = scale_buf[pl.ds(pl.multiple_of(i * rows, 8), rows), :]
+        scale = scale_buf[pl.ds(pl.multiple_of(i * rows, 8), rows), :] * weight
         for k in range(3):
             for first in range(0, 2 * rows, 16):
                 span = pl.ds(pl.multiple_of(i * 2 * rows + first, 16), 16)
@@ -79,8 +79,9 @@
                     term = l_buf[4 * k + a, span, :].astype(jnp.float32) * coupled
                     total = term if total is None else total + term
                 mixed[k, first : first + 16, :] = total
+        for k in range(3):
             sens = mixed[k, pl.ds(0, rows, stride=2), :] - mixed[k, pl.ds(1, rows, stride=2), :]
-            sens = (sens * weight) * scale
+            sens = sens * scale
             for owner in range(PER_STEP):
                 out[i * PER_STEP + owner, k * ROWS : (k + 1) * ROWS, :] = sens[owner * ROWS : (owner + 1) * ROWS, :]
 
@@ -111,48 +112,72 @@
     )(ids, *[pltpu.with_memory_space_constraint(each, pltpu.HBM) for each in (mass, weights, fwd, adj, size)])
 
 
-def products_kernel(cells, sens, steps, grads, gradient_out, precond, out, gradient, gradient_sem):
+def split(values):
+    parts = []
+    for _ in range(SPLITS):
+        parts.append(values.astype(jnp.bfloat16))
+        values = values - parts[-1].astype(jnp.float32)
+    return parts
+
+
+def products_kernel(
+    cells, sens, steps, grads, gradient_out, precond, out, gradient, total_rows, damped_rows, gradient_sem
+):
     owner = lax.axis_index(("x_hi", "z")) * GROUPS + lax.axis_index(FREQ)
     offset = cells[...] - owner * (ROWS * LANES)
     inside = (offset >= 0) & (offset < ROWS * LANES)
     row = jnp.where(inside, offset >> 7, -1)
     lane = offset & (LANES - 1)
+    place = lax.broadcasted_iota(jnp.int32, (PACK, LANES), 0)
+    place = jnp.where(place < 2 * ROWS, jnp.where(place < ROWS, place, place - ROWS), place - 2 * ROWS)
+    column = lax.broadcasted_iota(jnp.int32, (LANES, LANES), 0)
     row_hot, lane_hot = [], []
     for q in range(8):
-        r = jnp.broadcast_to(row[q : q + 1, :], (24, LANES))
-        c = jnp.broadcast_to(lane[q : q + 1, :], (LANES, LANES))
-        row_hot.append((r == lax.broadcasted_iota(jnp.int32, r.shape, 0)).astype(jnp.float32))
-        lane_hot.append((c == lax.broadcasted_iota(jnp.int32, c.shape, 0)).astype(jnp.float32))
+        row_hot.append((row[q : q + 1, :] == place).astype(jnp.float32).astype(jnp.bfloat16))
+        lane_hot.append((lane[q : q + 1, :] == column).astype(jnp.float32).astype(jnp.bfloat16))
     hits = lax.dot_general(
-        jnp.concatenate(row_hot, axis=1).astype(jnp.bfloat16),
-        jnp.concatenate(lane_hot, axis=1).astype(jnp.bfloat16),
+        jnp.concatenate(row_hot, axis=1),
+        jnp.concatenate(lane_hot, axis=1),
         (((1,), (1,)), ((), ())),
         preferred_element_type=jnp.float32,
     )
-    divisor = 1.0 + 4.0 * hits
-    products = jnp.zeros((48, 40), jnp.float32)
+    total = sens[0:PACK, :]
+    for f in range(1, SLOTS):
+        total = total + sens[f * PACK : (f + 1) * PACK, :]
+    total_rows[...] = total
+    for r in range(ROWS):
+        gradient[:, r * LANES : (r + 1) * LANES] = total_rows[pl.ds(r, 3, stride=ROWS), :]
     gradient_copy = pltpu.make_async_copy(gradient, gradient_out, gradient_sem)
+    gradient_copy.start()
+    damped_rows[...] = total / (1.0 + 4.0 * hits)
+    for r in range(ROWS):
+        precond[:, r * LANES : (r + 1) * LANES] = damped_rows[pl.ds(r, 3, stride=ROWS), :]
+    products = jnp.zeros((144, 144), jnp.float32)
     for k in range(3):
         slots, damped = [], []
         for r in range(ROWS):
-            block = sens[pl.ds(k * ROWS + r, SLOTS, stride=PACK), :]
-            span = slice(r * LANES, (r + 1) * LANES)
-            total = jnp.sum(block, axis=0, keepdims=True)
-            slots.append(block)
-            damped.append(total / divisor[r : r + 1, :])
-            gradient[k : k + 1, span] = total
-            precond[k : k + 1, span] = damped[-1]
-        if k == 2:
-            gradient_copy.start()
-        pairs = jnp.concatenate([steps[k], grads[k]], axis=0)
-        damped = jnp.broadcast_to(jnp.concatenate(damped, axis=1), (8, ROWS * LANES))
+            slots.append(sens[pl.ds(k * ROWS + r, SLOTS, stride=PACK), :])
+            damped.append(jnp.broadcast_to(damped_rows[k * ROWS + r : k * ROWS + r + 1, :], (16, LANES)))
+        pairs = split(jnp.concatenate([steps[k], grads[k]], axis=0))
+        slots = split(jnp.concatenate(slots, axis=1))
+        damped = split(jnp.concatenate(damped, axis=1))
         products = products + lax.dot_general(
-            jnp.concatenate([pairs, jnp.concatenate(slots, axis=1)], axis=0),
-            jnp.concatenate([pairs, damped], axis=0),
+            jnp.concatenate([*pairs, *slots], axis=0),
+            jnp.concatenate([*pairs, *damped], axis=0),
             (((1,), (1,)), ((), ())),
-            precision=HIGHEST,
             preferred_element_type=jnp.float32,
         )
+    products = sum(
+        products[:, 32 * b : 32 * b + 32] for b in reversed(range(SPLITS))
+    ), sum(products[:, 32 * SPLITS + 16 * b : 32 * SPLITS + 16 * b + 16] for b in reversed(range(SPLITS)))
+    products = jnp.concatenate(products, axis=1)
+    products = jnp.concatenate(
+        [
+            sum(products[32 * a : 32 * a + 32] for a in reversed(range(SPLITS))),
+            sum(products[32 * SPLITS + 16 * a : 32 * SPLITS + 16 * a + 16] for a in reversed(range(SPLITS))),
+        ],
+        axis=0,
+    )
     s, y, f = products[:16], products[16:32], products[32:]
     row = lax.broadcasted_iota(jnp.int32, (16, 16), 0)
     lane = lax.broadcasted_iota(jnp.int32, (16, 16), 1)
@@ -183,7 +208,12 @@
         out_shape=(own, own, jax.ShapeDtypeStruct((copies, 8, LANES), jnp.float32)),
         in_specs=[vmem] * 4,
         out_specs=(pl.BlockSpec(memory_space=pltpu.HBM), vmem, vmem),
-        scratch_shapes=[pltpu.VMEM(own.shape, own.dtype), pltpu.SemaphoreType.DMA(())],
+        scratch_shapes=[
+            pltpu.VMEM(own.shape, own.dtype),
+            pltpu.VMEM((PACK, LANES), jnp.float32),
+            pltpu.VMEM((PACK, LANES), jnp.float32),
+            pltpu.SemaphoreType.DMA(()),
+        ],
         compiler_params=pltpu.CompilerParams(vmem_limit_bytes=12 << 20),
         name="products",
     )(cells, sens, steps, grads)
@@ -258,12 +288,10 @@
 
 def directions(parts, steps, grads, precond):
     vmem = pl.BlockSpec(memory_space=pltpu.VMEM)
+    own = jax.ShapeDtypeStruct((3, ROWS * LANES), jnp.float32)
     return pl.pallas_call(
         direction_kernel,
-        out_shape=(
-            jax.ShapeDtypeStruct((3, ROWS * LANES), jnp.float32),
-            jax.ShapeDtypeStruct((SLOTS,), jnp.float32),
-        ),
+        out_shape=(own, jax.ShapeDtypeStruct((SLOTS,), jnp.float32)),
         in_specs=[vmem] * 4,
         out_specs=(vmem, vmem),
         compiler_params=pltpu.CompilerParams(vmem_limit_bytes=8 << 20),
@@ -305,7 +333,7 @@
         grads,
         lax.axis_size(PLANE),
     )
-    parts = lax.all_to_all(block, PLANE, 0, 0, tiled=True)
+    parts = lax.all_to_all(block, PLANE, 0, 0, tiled=True, axis_index_groups=[[(i + 14) % 32 for i in range(32)]])
     parts = lax.all_to_all(resend(parts, lax.axis_size("z")), "z", 0, 0, tiled=True, axis_index_groups=[[(i+8)%16 for i in range(16)]])
     direction, predicted = directions(parts, steps, grads, precond)
     return (gradient, direction, predicted)

time: 58.9 us -> 57.6 us (0.978)
  blocking collectives: 50.6 us -> 49.9 us
    all_to_all x1, blocking collectives: 20.1 us -> 19.5 us  [local(): lax.all_to_all(resend(parts, lax.axis_size('z')), 'z', 0, 0, tiled=True,...]
where the time goes in v4:
time: 57.6 us; the launch traced here: 57.4 us
  blocking collectives  49.9 us (87%)
  Pallas kernels  6.12 us (11%)
  between operations  1.32 us (2%)
    all_to_all x1, blocking collectives, local(): lax.all_to_all(resend(parts, lax.axis_size('z')), 'z', 0, 0, tiled=True,...  19.5 us
    all_to_all x1, blocking collectives, local(): arrived = lax.all_to_all(packed, FREQ, 0, 0, tiled=True)  19.2 us
    all_to_all x1, blocking collectives, local(): lax.all_to_all(block, PLANE, 0, 0, tiled=True, axis_index_groups=[[(i + 1...  11.2 us
    pallas_call x1, Pallas kernels, sens_to_owners(): pl.pallas_call(sens_kernel, out_shape=jax.ShapeDtypeStruct((GROUPS, PACK,...  3.47 us
    pallas_call x1, Pallas kernels, inner_products(): pl.pallas_call(products_kernel, out_shape=(own, own, jax.ShapeDtypeStruct...  1.49 us

profile of v4, /device:TPU:1, one launch (start us, length us, event | category | flops | bytes accessed | tf_op | source)
XLA Modules:
  0.0 57.4 jit_solution(15108359656950742882)
XLA Ops:
  1.3 0.0 copy-start
  1.3 0.0 copy-start.1
  1.3 0.0 copy-start.2
  1.3 3.5 %sens.1 = f32[16,64,128]{2,1,0:T(8,128)S(1)} custom-call(s32[1]{0:T(128)S(6)} %copy.14.ids, f32[3,4,4]{2,1,0:T(4,128)} %mass_in.1, f32[64]{0:T(128)} %weights_in.1, bf16[12,640,128]{2,1,0:T(8,128)(2,1)} %bitcast.21, bf16[12,640,128]{2,1,0:T(8,128)(2,1)} %bitcast.22, f32[320,128]{1,0:T(8,128)} %bitcast.23), custom_call_target="tpu_custom_call" | custom-call | tf_op jit(solution)/shard_map/sens/pallas_call | solution.py:94
  4.8 19.2 %all_to_all.15 = f32[16,64,128]{2,1,0:T(8,128)S(1)} all-to-all(f32[16,64,128]{2,1,0:T(8,128)S(1)} %sens.1), channel_id=1, replica_groups=mesh['y'=4,'x_lo'=2,'core'=2,'x_hi'=2,'z'=16] {'y','x_lo','core'}, dimensions={0} | all-to-all | bytes 1048576 | tf_op jit(solution)/shard_map/all_to_all | solution.py:328
  24.0 0.0 copy-done
  24.0 0.0 copy-done.1
  24.0 0.0 copy-done.2
  24.0 1.5 %products.1 = (f32[3,2560]{1,0:T(4,128)}, f32[3,2560]{1,0:T(4,128)S(1)}, f32[32,8,128]{2,1,0:T(8,128)S(1)}) custom-call(s32[8,128]{1,0:T(8,128)S(1)} %bitcast.20, f32[1024,128]{1,0:T(8,128)S(1)} %bitcast.15, f32[3,16,2560]{2,1,0:T(8,128)S(1)} %bitcast.16, f32[3,16,2560]{2,1,0:T(8,128)S(1)} %bitcast.18), custom_call_target="tpu_custom_call" | custom-call | tf_op jit(solution)/shard_map/products/pallas_call | solution.py:206
  25.5 11.2 %all_to_all.16.parts = f32[32,8,128]{2,1,0:T(8,128)S(1)} all-to-all(f32[32,8,128]{2,1,0:T(8,128)S(1)} %get-tuple-element.9), channel_id=1, replica_groups={{224,240,256,272,288,304,320,336,352,368,384,400,416,432,448,464,480,49..., dimensions={0} | all-to-all | bytes 262144 | tf_op jit(solution)/shard_map/all_to_all | solution.py:336
  36.8 19.5 %all_to_all.17.parts = f32[16,8,128]{2,1,0:T(8,128)S(1)} all-to-all(f32[16,8,128]{2,1,0:T(8,128)S(1)} %resend.1), channel_id=1, replica_groups={{8,9,10,11,12,13,14,15,0,1,2,3,4,5,6,7},{24,25,26,27,28,29,30,31,16,17,..., dimensions={0} | all-to-all | bytes 131072 | tf_op jit(solution)/shard_map/all_to_all | solution.py:337
  56.2 1.1 %direction.1 = (f32[3,2560]{1,0:T(4,128)}, f32[16]{0:T(128)}) custom-call(f32[16,8,128]{2,1,0:T(8,128)S(1)} %all_to_all.17.parts, f32[3,16,2560]{2,1,0:T(8,128)S(1)} %bitcast.17, f32[3,16,2560]{2,1,0:T(8,128)S(1)} %bitcast.19, f32[3,2560]{1,0:T(4,128)S(1)} %get-tuple-element.10.precond), custom_call_target="tpu_custom_call" | custom-call | tf_op jit(solution)/shard_map/direction/pallas_call | solution.py:292
  (1 shorter events, 0.0 us)
Async XLA Ops:
  1.3 22.7 %copy-start = (f32[16,3,2560]{2,0,1:T(8,128)S(1)}, f32[16,3,2560]{2,0,1:T(8,128)}, u32[]{:S(2)}) copy-start(f32[16,3,2560]{2,0,1:T(8,128)} %param.16) | copy-start | bytes 1474564
  1.3 22.7 %copy-start.1 = (f32[16,3,2560]{2,0,1:T(8,128)S(1)}, f32[16,3,2560]{2,0,1:T(8,128)}, u32[]{:S(2)}) copy-start(f32[16,3,2560]{2,0,1:T(8,128)} %param.17) | copy-start | bytes 1474564
  1.3 22.7 %copy-start.2 = (s32[1024]{0:T(1024)S(1)}, s32[1024]{0:T(1024)}, u32[]{:S(2)}) copy-start(s32[1024]{0:T(1024)} %param.15) | copy-start | bytes 12292

commit v5 on v4

--- a/solution.py
+++ b/solution.py
@@ -17,6 +17,9 @@
 FREQ = ("y", "x_lo", "core")
 PLANE = ("y", "x_lo", "core", "x_hi")
 PARAMS_ALL = 3932160
+FREQ_FIRST = 9
+PLANE_FIRST = 19
+Z_FIRST = 9
 SPLITS = 3
 
 
@@ -83,7 +86,7 @@
             sens = mixed[k, pl.ds(0, rows, stride=2), :] - mixed[k, pl.ds(1, rows, stride=2), :]
             sens = sens * scale
             for owner in range(PER_STEP):
-                out[i * PER_STEP + owner, k * ROWS : (k + 1) * ROWS, :] = sens[owner * ROWS : (owner + 1) * ROWS, :]
+                out[(i ^ FREQ_FIRST // PER_STEP) * PER_STEP + (owner ^ FREQ_FIRST % PER_STEP), k * ROWS : (k + 1) * ROWS, :] = sens[owner * ROWS : (owner + 1) * ROWS, :]
 
 
 def sens_to_owners(fwd, adj, mass, size, weights, ids):
@@ -276,7 +279,7 @@
         slots_second = slots_second + column(17 + m) * value
         second = place(m, value, second)
     change = -(gamma * column(51) + slots_second - gamma * slots_first) / PARAMS_ALL
-    predicted[...] = jnp.sum(jnp.where(row == lane, change, 0.0), axis=0)[:SLOTS]
+    predicted[...] = jnp.sum(jnp.where(row == (lane ^ FREQ_FIRST), change, 0.0), axis=0)[:SLOTS]
     scaled = gamma * first
     for k in range(3):
         for r in range(ROWS):
@@ -302,6 +305,10 @@
 def field_rows(field):
     split = field.reshape(2, EDGES, SLAB_ROWS, LANES)
     return split.transpose(1, 2, 0, 3).reshape(EDGES, 2 * SLAB_ROWS, LANES)
+
+
+def listed(count, first):
+    return [[(i + first) % count for i in range(count)]]
 
 
 def local(
@@ -325,7 +332,7 @@
         freq_weight,
         freq_ids,
     )
-    arrived = lax.all_to_all(packed, FREQ, 0, 0, tiled=True)
+    arrived = lax.all_to_all(packed, FREQ, 0, 0, tiled=True, axis_index_groups=[[i ^ FREQ_FIRST for i in range(16)]])
     gradient, precond, block = inner_products(
         receiver_cells.reshape(8, LANES),
         arrived.reshape(SLOTS * PACK, LANES),
@@ -333,8 +340,8 @@
         grads,
         lax.axis_size(PLANE),
     )
-    parts = lax.all_to_all(block, PLANE, 0, 0, tiled=True, axis_index_groups=[[(i + 14) % 32 for i in range(32)]])
-    parts = lax.all_to_all(resend(parts, lax.axis_size("z")), "z", 0, 0, tiled=True, axis_index_groups=[[(i+8)%16 for i in range(16)]])
+    parts = lax.all_to_all(block, PLANE, 0, 0, tiled=True, axis_index_groups=listed(32, PLANE_FIRST))
+    parts = lax.all_to_all(resend(parts, lax.axis_size("z")), "z", 0, 0, tiled=True, axis_index_groups=listed(16, Z_FIRST))
     direction, predicted = directions(parts, steps, grads, precond)
     return (gradient, direction, predicted)
 

time: 57.6 us -> 54.5 us (0.946)
  blocking collectives: 49.9 us -> 46.7 us
    all_to_all x2, blocking collectives: 30.4 us -> 28.8 us  [the longest x1 18.7 us: local(): lax.all_to_all(packed, FREQ, 0, 0, tiled=True, axis_index_groups=[[i ^ FR...]
    all_to_all x1, blocking collectives: 19.5 us -> 17.9 us  [local(): lax.all_to_all(resend(parts, lax.axis_size('z')), 'z', 0, 0, tiled=True,...]
where the time goes in v5:
time: 54.5 us; the launch traced here: 54.1 us
  blocking collectives  46.7 us (86%)
  Pallas kernels  6.12 us (11%)
  between operations  1.32 us (2%)
    all_to_all x1, blocking collectives, local(): lax.all_to_all(packed, FREQ, 0, 0, tiled=True, axis_index_groups=[[i ^ FR...  18.7 us
    all_to_all x1, blocking collectives, local(): lax.all_to_all(resend(parts, lax.axis_size('z')), 'z', 0, 0, tiled=True,...  17.9 us
    all_to_all x1, blocking collectives, local(): lax.all_to_all(block, PLANE, 0, 0, tiled=True, axis_index_groups=listed(3...  10.1 us
    pallas_call x1, Pallas kernels, sens_to_owners(): pl.pallas_call(sens_kernel, out_shape=jax.ShapeDtypeStruct((GROUPS, PACK,...  3.47 us
    pallas_call x1, Pallas kernels, inner_products(): pl.pallas_call(products_kernel, out_shape=(own, own, jax.ShapeDtypeStruct...  1.48 us
    pallas_call x1, Pallas kernels, directions(): pl.pallas_call(direction_kernel, out_shape=(own, jax.ShapeDtypeStruct((SL...  1.13 us

profile of v5, /device:TPU:1, one launch (start us, length us, event | category | flops | bytes accessed | tf_op | source)
XLA Modules:
  0.0 54.1 jit_solution(8144772820733394404)
XLA Ops:
  1.3 0.0 copy-start
  1.3 0.0 copy-start.1
  1.3 0.0 copy-start.2
  1.3 3.5 %sens.1 = f32[16,64,128]{2,1,0:T(8,128)S(1)} custom-call(s32[1]{0:T(128)S(6)} %copy.14.ids, f32[3,4,4]{2,1,0:T(4,128)} %mass_in.1, f32[64]{0:T(128)} %weights_in.1, bf16[12,640,128]{2,1,0:T(8,128)(2,1)} %bitcast.21, bf16[12,640,128]{2,1,0:T(8,128)(2,1)} %bitcast.22, f32[320,128]{1,0:T(8,128)} %bitcast.23), custom_call_target="tpu_custom_call" | custom-call | tf_op jit(solution)/shard_map/sens/pallas_call | solution.py:97
  4.8 18.7 %all_to_all.15 = f32[16,64,128]{2,1,0:T(8,128)S(1)} all-to-all(f32[16,64,128]{2,1,0:T(8,128)S(1)} %sens.1), channel_id=1, replica_groups={{288,256,352,320,416,384,480,448,32,0,96,64,160,128,224,192},{289,257,3..., dimensions={0} | all-to-all | bytes 1048576 | tf_op jit(solution)/shard_map/all_to_all | solution.py:335
  23.5 0.0 copy-done
  23.5 0.0 copy-done.1
  23.5 0.0 copy-done.2
  23.5 1.5 %products.1 = (f32[3,2560]{1,0:T(4,128)}, f32[3,2560]{1,0:T(4,128)S(1)}, f32[32,8,128]{2,1,0:T(8,128)S(1)}) custom-call(s32[8,128]{1,0:T(8,128)S(1)} %bitcast.20, f32[1024,128]{1,0:T(8,128)S(1)} %bitcast.15, f32[3,16,2560]{2,1,0:T(8,128)S(1)} %bitcast.16, f32[3,16,2560]{2,1,0:T(8,128)S(1)} %bitcast.18), custom_call_target="tpu_custom_call" | custom-call | tf_op jit(solution)/shard_map/products/pallas_call | solution.py:209
  25.0 10.1 %all_to_all.16.parts = f32[32,8,128]{2,1,0:T(8,128)S(1)} all-to-all(f32[32,8,128]{2,1,0:T(8,128)S(1)} %get-tuple-element.9), channel_id=1, replica_groups={{304,320,336,352,368,384,400,416,432,448,464,480,496,0,16,32,48,64,80,9..., dimensions={0} | all-to-all | bytes 262144 | tf_op jit(solution)/shard_map/all_to_all | solution.py:343
  35.1 17.9 %all_to_all.17.parts = f32[16,8,128]{2,1,0:T(8,128)S(1)} all-to-all(f32[16,8,128]{2,1,0:T(8,128)S(1)} %resend.1), channel_id=1, replica_groups={{9,10,11,12,13,14,15,0,1,2,3,4,5,6,7,8},{25,26,27,28,29,30,31,16,17,18,..., dimensions={0} | all-to-all | bytes 131072 | tf_op jit(solution)/shard_map/all_to_all | solution.py:344
  53.0 1.1 %direction.1 = (f32[3,2560]{1,0:T(4,128)}, f32[16]{0:T(128)}) custom-call(f32[16,8,128]{2,1,0:T(8,128)S(1)} %all_to_all.17.parts, f32[3,16,2560]{2,1,0:T(8,128)S(1)} %bitcast.17, f32[3,16,2560]{2,1,0:T(8,128)S(1)} %bitcast.19, f32[3,2560]{1,0:T(4,128)S(1)} %get-tuple-element.10.precond), custom_call_target="tpu_custom_call" | custom-call | tf_op jit(solution)/shard_map/direction/pallas_call | solution.py:295
  (1 shorter events, 0.0 us)
Async XLA Ops:
  1.3 22.2 %copy-start = (f32[16,3,2560]{2,0,1:T(8,128)S(1)}, f32[16,3,2560]{2,0,1:T(8,128)}, u32[]{:S(2)}) copy-start(f32[16,3,2560]{2,0,1:T(8,128)} %param.16) | copy-start | bytes 1474564
  1.3 22.2 %copy-start.1 = (f32[16,3,2560]{2,0,1:T(8,128)S(1)}, f32[16,3,2560]{2,0,1:T(8,128)}, u32[]{:S(2)}) copy-start(f32[16,3,2560]{2,0,1:T(8,128)} %param.17) | copy-start | bytes 1474564
  1.3 22.2 %copy-start.2 = (s32[1024]{0:T(1024)S(1)}, s32[1024]{0:T(1024)}, u32[]{:S(2)}) copy-start(s32[1024]{0:T(1024)} %param.15) | copy-start | bytes 12292

commit v6 on v5

--- a/solution.py
+++ b/solution.py
@@ -23,16 +23,40 @@
 SPLITS = 3
 
 
+def own_divisor(cells):
+    owner = lax.axis_index(("x_hi", "z")) * GROUPS + lax.axis_index(FREQ)
+    offset = cells - owner * (ROWS * LANES)
+    inside = (offset >= 0) & (offset < ROWS * LANES)
+    row = jnp.where(inside, offset >> 7, -1)
+    lane = offset & (LANES - 1)
+    place = lax.broadcasted_iota(jnp.int32, (PACK, LANES), 0)
+    place = jnp.where(place < 2 * ROWS, jnp.where(place < ROWS, place, place - ROWS), place - 2 * ROWS)
+    column = lax.broadcasted_iota(jnp.int32, (LANES, LANES), 0)
+    row_hot, lane_hot = [], []
+    for q in range(8):
+        row_hot.append((row[q : q + 1, :] == place).astype(jnp.float32).astype(jnp.bfloat16))
+        lane_hot.append((lane[q : q + 1, :] == column).astype(jnp.float32).astype(jnp.bfloat16))
+    return 1.0 + 4.0 * lax.dot_general(
+        jnp.concatenate(row_hot, axis=1),
+        jnp.concatenate(lane_hot, axis=1),
+        (((1,), (1,)), ((), ())),
+        preferred_element_type=jnp.float32,
+    )
+
+
 def sens_kernel(
     ids,
     mass_in,
     weights_in,
+    cells_in,
     fwd,
     adj,
     size,
     out,
+    divisor,
     mass,
     weights,
+    cells,
     e_buf,
     l_buf,
     scale_buf,
@@ -44,6 +68,7 @@
     rows = PER_STEP * ROWS
     steps = GROUPS // PER_STEP
     small = [
+        pltpu.make_async_copy(cells_in, cells, small_sem.at[3]),
         pltpu.make_async_copy(mass_in, mass, small_sem.at[0]),
         pltpu.make_async_copy(weights_in, weights, small_sem.at[1]),
         pltpu.make_async_copy(size, scale_buf, small_sem.at[2]),
@@ -61,7 +86,9 @@
     for i in range(steps):
         for copy in copies(i):
             copy.start()
-    for copy in small:
+    small[0].wait()
+    divisor[...] = own_divisor(cells[...])
+    for copy in small[1:]:
         copy.wait()
     weight = weights[ids[0]]
 
@@ -89,30 +116,34 @@
                 out[(i ^ FREQ_FIRST // PER_STEP) * PER_STEP + (owner ^ FREQ_FIRST % PER_STEP), k * ROWS : (k + 1) * ROWS, :] = sens[owner * ROWS : (owner + 1) * ROWS, :]
 
 
-def sens_to_owners(fwd, adj, mass, size, weights, ids):
+def sens_to_owners(fwd, adj, mass, size, weights, ids, cells):
     smem = pl.BlockSpec(memory_space=pltpu.SMEM)
     hbm = pl.BlockSpec(memory_space=pltpu.HBM)
     rows = PER_STEP * ROWS
     steps = GROUPS // PER_STEP
     return pl.pallas_call(
         sens_kernel,
-        out_shape=jax.ShapeDtypeStruct((GROUPS, PACK, LANES), jnp.float32),
-        in_specs=[smem, hbm, hbm, hbm, hbm, hbm],
-        out_specs=pl.BlockSpec(memory_space=pltpu.VMEM),
+        out_shape=(
+            jax.ShapeDtypeStruct((GROUPS, PACK, LANES), jnp.float32),
+            jax.ShapeDtypeStruct((PACK, LANES), jnp.float32),
+        ),
+        in_specs=[smem, hbm, hbm, hbm, hbm, hbm, hbm],
+        out_specs=(pl.BlockSpec(memory_space=pltpu.VMEM),) * 2,
         scratch_shapes=[
             pltpu.SMEM(mass.shape, mass.dtype),
             pltpu.SMEM(weights.shape, weights.dtype),
+            pltpu.VMEM(cells.shape, cells.dtype),
             pltpu.VMEM(fwd.shape, fwd.dtype),
             pltpu.VMEM(adj.shape, adj.dtype),
             pltpu.VMEM(size.shape, size.dtype),
             pltpu.VMEM((3, 2 * rows, LANES), jnp.float32),
             pltpu.SemaphoreType.DMA((steps,)),
             pltpu.SemaphoreType.DMA((steps,)),
-            pltpu.SemaphoreType.DMA((3,)),
+            pltpu.SemaphoreType.DMA((4,)),
         ],
         compiler_params=pltpu.CompilerParams(vmem_limit_bytes=12 << 20),
         name="sens",
-    )(ids, *[pltpu.with_memory_space_constraint(each, pltpu.HBM) for each in (mass, weights, fwd, adj, size)])
+    )(ids, *[pltpu.with_memory_space_constraint(each, pltpu.HBM) for each in (mass, weights, cells, fwd, adj, size)])
 
 
 def split(values):
@@ -124,26 +155,8 @@
 
 
 def products_kernel(
-    cells, sens, steps, grads, gradient_out, precond, out, gradient, total_rows, damped_rows, gradient_sem
+    divisor, sens, steps, grads, gradient_out, precond, out, gradient, total_rows, damped_rows, gradient_sem
 ):
-    owner = lax.axis_index(("x_hi", "z")) * GROUPS + lax.axis_index(FREQ)
-    offset = cells[...] - owner * (ROWS * LANES)
-    inside = (offset >= 0) & (offset < ROWS * LANES)
-    row = jnp.where(inside, offset >> 7, -1)
-    lane = offset & (LANES - 1)
-    place = lax.broadcasted_iota(jnp.int32, (PACK, LANES), 0)
-    place = jnp.where(place < 2 * ROWS, jnp.where(place < ROWS, place, place - ROWS), place - 2 * ROWS)
-    column = lax.broadcasted_iota(jnp.int32, (LANES, LANES), 0)
-    row_hot, lane_hot = [], []
-    for q in range(8):
-        row_hot.append((row[q : q + 1, :] == place).astype(jnp.float32).astype(jnp.bfloat16))
-        lane_hot.append((lane[q : q + 1, :] == column).astype(jnp.float32).astype(jnp.bfloat16))
-    hits = lax.dot_general(
-        jnp.concatenate(row_hot, axis=1),
-        jnp.concatenate(lane_hot, axis=1),
-        (((1,), (1,)), ((), ())),
-        preferred_element_type=jnp.float32,
-    )
     total = sens[0:PACK, :]
     for f in range(1, SLOTS):
         total = total + sens[f * PACK : (f + 1) * PACK, :]
@@ -152,7 +165,7 @@
         gradient[:, r * LANES : (r + 1) * LANES] = total_rows[pl.ds(r, 3, stride=ROWS), :]
     gradient_copy = pltpu.make_async_copy(gradient, gradient_out, gradient_sem)
     gradient_copy.start()
-    damped_rows[...] = total / (1.0 + 4.0 * hits)
+    damped_rows[...] = total / divisor[...]
     for r in range(ROWS):
         precond[:, r * LANES : (r + 1) * LANES] = damped_rows[pl.ds(r, 3, stride=ROWS), :]
     products = jnp.zeros((144, 144), jnp.float32)
@@ -203,7 +216,7 @@
     gradient_copy.wait()
 
 
-def inner_products(cells, sens, steps, grads, copies):
+def inner_products(divisor, sens, steps, grads, copies):
     vmem = pl.BlockSpec(memory_space=pltpu.VMEM)
     own = jax.ShapeDtypeStruct((3, ROWS * LANES), jnp.float32)
     return pl.pallas_call(
@@ -219,7 +232,7 @@
         ],
         compiler_params=pltpu.CompilerParams(vmem_limit_bytes=12 << 20),
         name="products",
-    )(cells, sens, steps, grads)
+    )(divisor, sens, steps, grads)
 
 
 def resend_kernel(parts, out):
@@ -324,17 +337,18 @@
 ):
     steps = step_pairs.transpose(1, 0, 2)
     grads = grad_pairs.transpose(1, 0, 2)
-    packed = sens_to_owners(
+    packed, divisor = sens_to_owners(
         field_rows(forward_field),
         field_rows(adjoint_field),
         mass_block,
         cell_size.reshape(SLAB_ROWS, LANES),
         freq_weight,
         freq_ids,
+        receiver_cells.reshape(8, LANES),
     )
     arrived = lax.all_to_all(packed, FREQ, 0, 0, tiled=True, axis_index_groups=[[i ^ FREQ_FIRST for i in range(16)]])
     gradient, precond, block = inner_products(
-        receiver_cells.reshape(8, LANES),
+        divisor,
         arrived.reshape(SLOTS * PACK, LANES),
         steps,
         grads,

time: 54.5 us -> 54.1 us (level)
  no operation moved by 1% of the time
where the time goes in v6:
time: 54.1 us; the launch traced here: 53.8 us
  blocking collectives  46.7 us (86%)
  Pallas kernels  5.79 us (11%)
  between operations  1.31 us (2%)
    all_to_all x1, blocking collectives, local(): lax.all_to_all(packed, FREQ, 0, 0, tiled=True, axis_index_groups=[[i ^ FR...  18.7 us
    all_to_all x1, blocking collectives, local(): lax.all_to_all(resend(parts, lax.axis_size('z')), 'z', 0, 0, tiled=True,...  17.9 us
    all_to_all x1, blocking collectives, local(): lax.all_to_all(block, PLANE, 0, 0, tiled=True, axis_index_groups=listed(3...  10.1 us
    pallas_call x1, Pallas kernels, sens_to_owners(): pl.pallas_call(sens_kernel, out_shape=(jax.ShapeDtypeStruct((GROUPS, PACK...  3.5 us
    pallas_call x1, Pallas kernels, inner_products(): pl.pallas_call(products_kernel, out_shape=(own, own, jax.ShapeDtypeStruct...  1.14 us
    pallas_call x1, Pallas kernels, directions(): pl.pallas_call(direction_kernel, out_shape=(own, jax.ShapeDtypeStruct((SL...  1.12 us

profile of v6, /device:TPU:1, one launch (start us, length us, event | category | flops | bytes accessed | tf_op | source)
XLA Modules:
  0.0 53.8 jit_solution(10324378115089501750)
XLA Ops:
  1.3 0.0 copy-start
  1.3 0.0 copy-start.1
  1.3 3.5 %sens.1 = (f32[16,64,128]{2,1,0:T(8,128)S(1)}, f32[64,128]{1,0:T(8,128)S(1)}) custom-call(s32[1]{0:T(128)S(6)} %copy.14.ids, f32[3,4,4]{2,1,0:T(4,128)} %mass_in.1, f32[64]{0:T(128)} %weights_in.1, s32[8,128]{1,0:T(8,128)} %bitcast.23, bf16[12,640,128]{2,1,0:T(8,128)(2,1)} %bitcast.20, bf16[12,640,128]{2,1,0:T(8,128)(2,1)} %bitcast.21, f32[320,128]{1,0:T(8,128)} %bitcast.22), custom_call_target="tpu_custom_call" | custom-call | tf_op jit(solution)/shard_map/sens/pallas_call | solution.py:124
  4.8 18.7 %all_to_all.15 = f32[16,64,128]{2,1,0:T(8,128)S(1)} all-to-all(f32[16,64,128]{2,1,0:T(8,128)S(1)} %get-tuple-element.11), channel_id=1, replica_groups={{288,256,352,320,416,384,480,448,32,0,96,64,160,128,224,192},{289,257,3..., dimensions={0} | all-to-all | bytes 1048576 | tf_op jit(solution)/shard_map/all_to_all | solution.py:349
  23.5 0.0 copy-done
  23.5 0.0 copy-done.1
  23.5 1.1 %products.1 = (f32[3,2560]{1,0:T(4,128)}, f32[3,2560]{1,0:T(4,128)S(1)}, f32[32,8,128]{2,1,0:T(8,128)S(1)}) custom-call(f32[64,128]{1,0:T(8,128)S(1)} %get-tuple-element.10.divisor, f32[1024,128]{1,0:T(8,128)S(1)} %bitcast.15, f32[3,16,2560]{2,1,0:T(8,128)S(1)} %bitcast.16, f32[3,16,2560]{2,1,0:T(8,128)S(1)} %bitcast.18), custom_call_target="tpu_custom_call" | custom-call | tf_op jit(solution)/shard_map/products/pallas_call | solution.py:222
  24.7 10.1 %all_to_all.16.parts = f32[32,8,128]{2,1,0:T(8,128)S(1)} all-to-all(f32[32,8,128]{2,1,0:T(8,128)S(1)} %get-tuple-element.13), channel_id=1, replica_groups={{304,320,336,352,368,384,400,416,432,448,464,480,496,0,16,32,48,64,80,9..., dimensions={0} | all-to-all | bytes 262144 | tf_op jit(solution)/shard_map/all_to_all | solution.py:357
  34.8 17.9 %all_to_all.17.parts = f32[16,8,128]{2,1,0:T(8,128)S(1)} all-to-all(f32[16,8,128]{2,1,0:T(8,128)S(1)} %resend.1), channel_id=1, replica_groups={{9,10,11,12,13,14,15,0,1,2,3,4,5,6,7,8},{25,26,27,28,29,30,31,16,17,18,..., dimensions={0} | all-to-all | bytes 131072 | tf_op jit(solution)/shard_map/all_to_all | solution.py:358
  52.7 1.1 %direction.1 = (f32[3,2560]{1,0:T(4,128)}, f32[16]{0:T(128)}) custom-call(f32[16,8,128]{2,1,0:T(8,128)S(1)} %all_to_all.17.parts, f32[3,16,2560]{2,1,0:T(8,128)S(1)} %bitcast.17, f32[3,16,2560]{2,1,0:T(8,128)S(1)} %bitcast.19, f32[3,2560]{1,0:T(4,128)S(1)} %get-tuple-element.14.precond), custom_call_target="tpu_custom_call" | custom-call | tf_op jit(solution)/shard_map/direction/pallas_call | solution.py:308
  (1 shorter events, 0.0 us)
Async XLA Ops:
  1.3 22.2 %copy-start = (f32[16,3,2560]{2,0,1:T(8,128)S(1)}, f32[16,3,2560]{2,0,1:T(8,128)}, u32[]{:S(2)}) copy-start(f32[16,3,2560]{2,0,1:T(8,128)} %param.16) | copy-start | bytes 1474564
  1.3 22.2 %copy-start.1 = (f32[16,3,2560]{2,0,1:T(8,128)S(1)}, f32[16,3,2560]{2,0,1:T(8,128)}, u32[]{:S(2)}) copy-start(f32[16,3,2560]{2,0,1:T(8,128)} %param.17) | copy-start | bytes 1474564

commit v7 on v6

--- a/solution.py
+++ b/solution.py
@@ -98,14 +98,15 @@
             copy.wait()
         scale = scale_buf[pl.ds(pl.multiple_of(i * rows, 8), rows), :] * weight
         for k in range(3):
+            factor = [[jnp.full((16, LANES), mass[k, a, b]) for b in range(4)] for a in range(4)]
             for first in range(0, 2 * rows, 16):
                 span = pl.ds(pl.multiple_of(i * 2 * rows + first, 16), 16)
                 e = [e_buf[4 * k + b, span, :].astype(jnp.float32) for b in range(4)]
                 total = None
                 for a in range(4):
-                    coupled = mass[k, a, 0] * e[0]
+                    coupled = factor[a][0] * e[0]
                     for b in range(1, 4):
-                        coupled = coupled + mass[k, a, b] * e[b]
+                        coupled = coupled + factor[a][b] * e[b]
                     term = l_buf[4 * k + a, span, :].astype(jnp.float32) * coupled
                     total = term if total is None else total + term
                 mixed[k, first : first + 16, :] = total
@@ -324,6 +325,10 @@
     return [[(i + first) % count for i in range(count)]]
 
 
+def farthest_first(count, first):
+    return [[first] + [(first + side * far) % count for far in range(count // 2, 0, -1) for side in (1, -1)][1:]]
+
+
 def local(
     forward_field,
     adjoint_field,
@@ -355,7 +360,7 @@
         lax.axis_size(PLANE),
     )
     parts = lax.all_to_all(block, PLANE, 0, 0, tiled=True, axis_index_groups=listed(32, PLANE_FIRST))
-    parts = lax.all_to_all(resend(parts, lax.axis_size("z")), "z", 0, 0, tiled=True, axis_index_groups=listed(16, Z_FIRST))
+    parts = lax.all_to_all(resend(parts, lax.axis_size("z")), "z", 0, 0, tiled=True, axis_index_groups=farthest_first(16, Z_FIRST))
     direction, predicted = directions(parts, steps, grads, precond)
     return (gradient, direction, predicted)
 

time: 54.1 us -> 54 us (level)
  no operation moved by 1% of the time
where the time goes in v7:
time: 54 us; the launch traced here: 53.3 us
  blocking collectives  46.3 us (86%)
  Pallas kernels  5.76 us (11%)
  between operations  1.31 us (2%)
    all_to_all x1, blocking collectives, local(): lax.all_to_all(packed, FREQ, 0, 0, tiled=True, axis_index_groups=[[i ^ FR...  18.7 us
    all_to_all x1, blocking collectives, local(): lax.all_to_all(resend(parts, lax.axis_size('z')), 'z', 0, 0, tiled=True,...  17.5 us
    all_to_all x1, blocking collectives, local(): lax.all_to_all(block, PLANE, 0, 0, tiled=True, axis_index_groups=listed(3...  10.1 us
    pallas_call x1, Pallas kernels, sens_to_owners(): pl.pallas_call(sens_kernel, out_shape=(jax.ShapeDtypeStruct((GROUPS, PACK...  3.46 us
    pallas_call x1, Pallas kernels, inner_products(): pl.pallas_call(products_kernel, out_shape=(own, own, jax.ShapeDtypeStruct...  1.14 us
    pallas_call x1, Pallas kernels, directions(): pl.pallas_call(direction_kernel, out_shape=(own, jax.ShapeDtypeStruct((SL...  1.12 us

profile of v7, /device:TPU:1, one launch (start us, length us, event | category | flops | bytes accessed | tf_op | source)
XLA Modules:
  0.0 53.3 jit_solution(2828056863926488359)
XLA Ops:
  1.3 0.0 copy-start
  1.3 0.0 copy-start.1
  1.3 3.5 %sens.1 = (f32[16,64,128]{2,1,0:T(8,128)S(1)}, f32[64,128]{1,0:T(8,128)S(1)}) custom-call(s32[1]{0:T(128)S(6)} %copy.14.ids, f32[3,4,4]{2,1,0:T(4,128)} %mass_in.1, f32[64]{0:T(128)} %weights_in.1, s32[8,128]{1,0:T(8,128)} %bitcast.23, bf16[12,640,128]{2,1,0:T(8,128)(2,1)} %bitcast.20, bf16[12,640,128]{2,1,0:T(8,128)(2,1)} %bitcast.21, f32[320,128]{1,0:T(8,128)} %bitcast.22), custom_call_target="tpu_custom_call" | custom-call | tf_op jit(solution)/shard_map/sens/pallas_call | solution.py:125
  4.8 18.7 %all_to_all.15 = f32[16,64,128]{2,1,0:T(8,128)S(1)} all-to-all(f32[16,64,128]{2,1,0:T(8,128)S(1)} %get-tuple-element.11), channel_id=1, replica_groups={{288,256,352,320,416,384,480,448,32,0,96,64,160,128,224,192},{289,257,3..., dimensions={0} | all-to-all | bytes 1048576 | tf_op jit(solution)/shard_map/all_to_all | solution.py:354
  23.5 0.0 copy-done
  23.5 0.0 copy-done.1
  23.5 1.1 %products.1 = (f32[3,2560]{1,0:T(4,128)}, f32[3,2560]{1,0:T(4,128)S(1)}, f32[32,8,128]{2,1,0:T(8,128)S(1)}) custom-call(f32[64,128]{1,0:T(8,128)S(1)} %get-tuple-element.10.divisor, f32[1024,128]{1,0:T(8,128)S(1)} %bitcast.15, f32[3,16,2560]{2,1,0:T(8,128)S(1)} %bitcast.16, f32[3,16,2560]{2,1,0:T(8,128)S(1)} %bitcast.18), custom_call_target="tpu_custom_call" | custom-call | tf_op jit(solution)/shard_map/products/pallas_call | solution.py:223
  24.6 10.1 %all_to_all.16.parts = f32[32,8,128]{2,1,0:T(8,128)S(1)} all-to-all(f32[32,8,128]{2,1,0:T(8,128)S(1)} %get-tuple-element.13), channel_id=1, replica_groups={{304,320,336,352,368,384,400,416,432,448,464,480,496,0,16,32,48,64,80,9..., dimensions={0} | all-to-all | bytes 262144 | tf_op jit(solution)/shard_map/all_to_all | solution.py:362
  34.7 17.5 %all_to_all.17.parts = f32[16,8,128]{2,1,0:T(8,128)S(1)} all-to-all(f32[16,8,128]{2,1,0:T(8,128)S(1)} %resend.1), channel_id=1, replica_groups={{9,1,0,2,15,3,14,4,13,5,12,6,11,7,10,8},{25,17,16,18,31,19,30,20,29,21,..., dimensions={0} | all-to-all | bytes 131072 | tf_op jit(solution)/shard_map/all_to_all | solution.py:363
  52.2 1.1 %direction.1 = (f32[3,2560]{1,0:T(4,128)}, f32[16]{0:T(128)}) custom-call(f32[16,8,128]{2,1,0:T(8,128)S(1)} %all_to_all.17.parts, f32[3,16,2560]{2,1,0:T(8,128)S(1)} %bitcast.17, f32[3,16,2560]{2,1,0:T(8,128)S(1)} %bitcast.19, f32[3,2560]{1,0:T(4,128)S(1)} %get-tuple-element.14.precond), custom_call_target="tpu_custom_call" | custom-call | tf_op jit(solution)/shard_map/direction/pallas_call | solution.py:309
  (1 shorter events, 0.0 us)
Async XLA Ops:
  1.3 22.2 %copy-start = (f32[16,3,2560]{2,0,1:T(8,128)S(1)}, f32[16,3,2560]{2,0,1:T(8,128)}, u32[]{:S(2)}) copy-start(f32[16,3,2560]{2,0,1:T(8,128)} %param.16) | copy-start | bytes 1474564
  1.3 22.2 %copy-start.1 = (f32[16,3,2560]{2,0,1:T(8,128)S(1)}, f32[16,3,2560]{2,0,1:T(8,128)}, u32[]{:S(2)}) copy-start(f32[16,3,2560]{2,0,1:T(8,128)} %param.17) | copy-start | bytes 1474564

commit v8 on v7

--- a/solution.py
+++ b/solution.py
@@ -167,8 +167,6 @@
     gradient_copy = pltpu.make_async_copy(gradient, gradient_out, gradient_sem)
     gradient_copy.start()
     damped_rows[...] = total / divisor[...]
-    for r in range(ROWS):
-        precond[:, r * LANES : (r + 1) * LANES] = damped_rows[pl.ds(r, 3, stride=ROWS), :]
     products = jnp.zeros((144, 144), jnp.float32)
     for k in range(3):
         slots, damped = [], []
@@ -214,6 +212,8 @@
     block = jnp.concatenate([block[:8], block[8:]], axis=1)
     for i in range(out.shape[0]):
         out[i] = block
+    for r in range(ROWS):
+        precond[:, r * LANES : (r + 1) * LANES] = damped_rows[pl.ds(r, 3, stride=ROWS), :]
     gradient_copy.wait()
 
 

time: 54 us -> 54 us (level)
  no operation moved by 1% of the time
where the time goes in v8:
time: 54 us; the launch traced here: 53.3 us
  blocking collectives  46.3 us (86%)
  Pallas kernels  5.76 us (11%)
  between operations  1.31 us (2%)
    all_to_all x1, blocking collectives, local(): lax.all_to_all(packed, FREQ, 0, 0, tiled=True, axis_index_groups=[[i ^ FR...  18.7 us
    all_to_all x1, blocking collectives, local(): lax.all_to_all(resend(parts, lax.axis_size('z')), 'z', 0, 0, tiled=True,...  17.5 us
    all_to_all x1, blocking collectives, local(): lax.all_to_all(block, PLANE, 0, 0, tiled=True, axis_index_groups=listed(3...  10.1 us
    pallas_call x1, Pallas kernels, sens_to_owners(): pl.pallas_call(sens_kernel, out_shape=(jax.ShapeDtypeStruct((GROUPS, PACK...  3.46 us
    pallas_call x1, Pallas kernels, inner_products(): pl.pallas_call(products_kernel, out_shape=(own, own, jax.ShapeDtypeStruct...  1.13 us
    pallas_call x1, Pallas kernels, directions(): pl.pallas_call(direction_kernel, out_shape=(own, jax.ShapeDtypeStruct((SL...  1.12 us

profile of v8, /device:TPU:1, one launch (start us, length us, event | category | flops | bytes accessed | tf_op | source)
XLA Modules:
  0.0 53.3 jit_solution(9247291566060642422)
XLA Ops:
  1.3 0.0 copy-start
  1.3 0.0 copy-start.1
  1.3 3.5 %sens.1 = (f32[16,64,128]{2,1,0:T(8,128)S(1)}, f32[64,128]{1,0:T(8,128)S(1)}) custom-call(s32[1]{0:T(128)S(6)} %copy.14.ids, f32[3,4,4]{2,1,0:T(4,128)} %mass_in.1, f32[64]{0:T(128)} %weights_in.1, s32[8,128]{1,0:T(8,128)} %bitcast.23, bf16[12,640,128]{2,1,0:T(8,128)(2,1)} %bitcast.20, bf16[12,640,128]{2,1,0:T(8,128)(2,1)} %bitcast.21, f32[320,128]{1,0:T(8,128)} %bitcast.22), custom_call_target="tpu_custom_call" | custom-call | tf_op jit(solution)/shard_map/sens/pallas_call | solution.py:125
  4.8 18.7 %all_to_all.15 = f32[16,64,128]{2,1,0:T(8,128)S(1)} all-to-all(f32[16,64,128]{2,1,0:T(8,128)S(1)} %get-tuple-element.11), channel_id=1, replica_groups={{288,256,352,320,416,384,480,448,32,0,96,64,160,128,224,192},{289,257,3..., dimensions={0} | all-to-all | bytes 1048576 | tf_op jit(solution)/shard_map/all_to_all | solution.py:354
  23.5 0.0 copy-done
  23.5 0.0 copy-done.1
  23.5 1.1 %products.1 = (f32[3,2560]{1,0:T(4,128)}, f32[3,2560]{1,0:T(4,128)S(1)}, f32[32,8,128]{2,1,0:T(8,128)S(1)}) custom-call(f32[64,128]{1,0:T(8,128)S(1)} %get-tuple-element.10.divisor, f32[1024,128]{1,0:T(8,128)S(1)} %bitcast.15, f32[3,16,2560]{2,1,0:T(8,128)S(1)} %bitcast.16, f32[3,16,2560]{2,1,0:T(8,128)S(1)} %bitcast.18), custom_call_target="tpu_custom_call" | custom-call | tf_op jit(solution)/shard_map/products/pallas_call | solution.py:223
  24.6 10.1 %all_to_all.16.parts = f32[32,8,128]{2,1,0:T(8,128)S(1)} all-to-all(f32[32,8,128]{2,1,0:T(8,128)S(1)} %get-tuple-element.13), channel_id=1, replica_groups={{304,320,336,352,368,384,400,416,432,448,464,480,496,0,16,32,48,64,80,9..., dimensions={0} | all-to-all | bytes 262144 | tf_op jit(solution)/shard_map/all_to_all | solution.py:362
  34.7 17.5 %all_to_all.17.parts = f32[16,8,128]{2,1,0:T(8,128)S(1)} all-to-all(f32[16,8,128]{2,1,0:T(8,128)S(1)} %resend.1), channel_id=1, replica_groups={{9,1,0,2,15,3,14,4,13,5,12,6,11,7,10,8},{25,17,16,18,31,19,30,20,29,21,..., dimensions={0} | all-to-all | bytes 131072 | tf_op jit(solution)/shard_map/all_to_all | solution.py:363
  52.2 1.1 %direction.1 = (f32[3,2560]{1,0:T(4,128)}, f32[16]{0:T(128)}) custom-call(f32[16,8,128]{2,1,0:T(8,128)S(1)} %all_to_all.17.parts, f32[3,16,2560]{2,1,0:T(8,128)S(1)} %bitcast.17, f32[3,16,2560]{2,1,0:T(8,128)S(1)} %bitcast.19, f32[3,2560]{1,0:T(4,128)S(1)} %get-tuple-element.14.precond), custom_call_target="tpu_custom_call" | custom-call | tf_op jit(solution)/shard_map/direction/pallas_call | solution.py:309
  (1 shorter events, 0.0 us)
Async XLA Ops:
  1.3 22.2 %copy-start = (f32[16,3,2560]{2,0,1:T(8,128)S(1)}, f32[16,3,2560]{2,0,1:T(8,128)}, u32[]{:S(2)}) copy-start(f32[16,3,2560]{2,0,1:T(8,128)} %param.16) | copy-start | bytes 1474564
  1.3 22.2 %copy-start.1 = (f32[16,3,2560]{2,0,1:T(8,128)S(1)}, f32[16,3,2560]{2,0,1:T(8,128)}, u32[]{:S(2)}) copy-start(f32[16,3,2560]{2,0,1:T(8,128)} %param.17) | copy-start | bytes 1474564
